TPU v7x, 32 devices: a whole 2x2x4 slice. The times are simulated.
32 devices in a mesh: tm: 8 (over z, y), height: 4 (over x, core).
Axes of the slice: x: 2, y: 2, z: 4, core: 2. Of those that a mesh axis runs over, the one named last changes fastest.
Arguments:
- latents: bfloat16 [16, 16, 128, 256], P('tm', 'height'), may hold values from -6 to 6
- conv_first: bfloat16 [3, 3, 3, 256, 256], replicated, may hold values from -0.078125 to 0.078125
- conv_second: bfloat16 [3, 3, 3, 256, 256], replicated, may hold values from -0.078125 to 0.078125
- codebook: bfloat16 [262144, 256], P('height'), may hold values from -13 to 13
- codes: int32 [16, 16, 128], P('tm', 'height'), may hold values from 0 to 262143, as said below
- upstream: bfloat16 [16, 16, 128, 256], P('tm', 'height'), may hold values from -6 to 6
Outputs:
- grad_latent: bfloat16 [16, 16, 128, 256], P('tm', 'height')
- codebook_grad: bfloat16 [262144, 256], P(('height', 'tm'))
Inputs may be any that keep to these rules, and one draw needn't show every extreme that they name: Each device's 1024 cells hold at most 64 codes of any one aligned range of 8192 codes; some ranges receive exactly 64 from every device.
All inputs are finite; a program needn't handle non-finite values.
Results may differ from a plain program's by a relative error of at most 0.0085.
Values may be sent and summed in bfloat16 or wider, within the bound.
No kernel may reach another device: no remote copies, remote signals or barrier semaphores. Data moves between devices by JAX's collectives and lax.ppermute only.
A program may use at most 128 MiB of HBM per device.

v0:
```python
import functools

import jax
import jax.numpy as jnp
from jax import lax
from jax.experimental import pallas as pl
from jax.experimental.pallas import tpu as pltpu
from jax.sharding import PartitionSpec as P

COMMIT = 0.25
BATCH = 64
TILE = 16
BLOCK = 256
F32 = jnp.float32
BF16 = jnp.bfloat16
VMEM = pl.BlockSpec(memory_space=pltpu.VMEM)
SMEM = pl.BlockSpec(memory_space=pltpu.SMEM)
HBM = pl.BlockSpec(memory_space=pltpu.MemorySpace.HBM)
NT = (((1,), (1,)), ((), ()))


def along(x, axis, by):
    count = lax.axis_size(axis)
    return lax.ppermute(x, axis, [(i, i + by) for i in range(count) if 0 <= i + by < count])


def around(x, axis, by):
    count = lax.axis_size(axis)
    return lax.ppermute(x, axis, [(i, (i + by) % count) for i in range(count)])


def params(megabytes=28):
    return pltpu.CompilerParams(vmem_limit_bytes=megabytes << 20)


def act(values):
    scaled = values * lax.rsqrt(jnp.mean(values * values, -1, keepdims=True) + 1e-06)
    return scaled / (1.0 + jnp.exp(-scaled))


def lanes(block):
    return jnp.concatenate([block[i : i + 1, :] for i in range(block.shape[0])], axis=1)


def fetch(pairs, sems):
    copies = [pltpu.make_async_copy(src, dst, sems.at[i]) for i, (src, dst) in enumerate(pairs)]
    for copy in copies:
        copy.start()
    return copies


def finish(copies):
    for copy in copies:
        copy.wait()


def onehot(mask):
    return jnp.where(mask, 1.0, 0.0).astype(BF16)


def index_kernel(groups, tiles, held, capacity, here_ref, codes_ref, send_ref, place_ref):
    lines, width = codes_ref.shape
    cells = lines * width
    owners = groups * tiles
    range_rows = held // tiles
    block_slots = tiles * capacity
    near, here = here_ref[0], here_ref[1]
    own = lanes(codes_ref[...])
    block = own // range_rows
    target = block % tiles * groups + block // tiles
    home = own // held
    own_hits = lax.broadcasted_iota(jnp.int32, (owners, cells), 0) == target
    home_hits = lax.broadcasted_iota(jnp.int32, (groups, cells), 0) == home
    pad = -(owners + groups) % 16
    hits = jnp.concatenate(
        [jnp.where(own_hits, 1.0, 0.0), jnp.where(home_hits, 1.0, 0.0), jnp.zeros((pad, cells), F32)], axis=0
    )
    earlier = onehot(
        lax.broadcasted_iota(jnp.int32, (width, width), 0) < lax.broadcasted_iota(jnp.int32, (width, width), 1)
    )
    before = jnp.zeros((hits.shape[0], 1), F32)
    parts = []
    for i in range(lines):
        part = hits[:, i * width : (i + 1) * width]
        parts.append(jnp.dot(part.astype(BF16), earlier, preferred_element_type=F32) + before)
        before = before + jnp.sum(part, 1, keepdims=True)
    ranks = hits * jnp.concatenate(parts, axis=1)
    own_rank = jnp.sum(ranks[:owners], 0, keepdims=True)
    home_rank = jnp.sum(ranks[owners : owners + groups], 0, keepdims=True)
    arrival = lax.rem(here - home + groups, groups)
    place_ref[0:1, :] = target.astype(F32) * capacity + own_rank
    place_ref[1:2, :] = arrival.astype(F32) * block_slots + home_rank
    place_ref[2:, :] = jnp.zeros((6, cells), F32)
    send_ref[...] = jnp.zeros(send_ref.shape, jnp.int32)

    def spread(ones, code, rank):
        count = ones.shape[0]
        high, low = (code // 256).astype(F32), (code % 256).astype(F32)
        picked = jnp.concatenate([ones * high, ones * low, ones], axis=0).astype(BF16)
        chosen = onehot(lax.broadcasted_iota(jnp.int32, (width, cells), 0) == rank)
        out = lax.dot_general(picked, chosen, NT, preferred_element_type=F32)
        code = out[:count] * 256.0 + out[count : 2 * count]
        return jnp.where(out[2 * count :] > 0.5, code, -1.0).astype(jnp.int32)

    send_ref[:, 7, :] = spread(hits[:owners], own % range_rows, own_rank.astype(jnp.int32))
    asked_lines = block_slots // width
    line = home_rank.astype(jnp.int32) // width
    for h in range(groups):
        ones = jnp.where(
            (lax.broadcasted_iota(jnp.int32, (8, cells), 0) == line) & (home == h), 1.0, 0.0
        )
        asked = spread(ones, own % held, home_rank.astype(jnp.int32) % width)
        send_ref[near * groups + h, 0:asked_lines, :] = asked[:asked_lines]


def gather_kernel(groups, here_ref, asked_ref, book_ref, _, *refs):
    outs, (done, ask, lows, land, out, sems, out_sems) = refs[:groups], refs[groups:]
    done[...] = jnp.zeros_like(done)
    rows, width = ask.shape
    near, here = here_ref[0], here_ref[1]
    mine = asked_ref.at[pl.ds(pl.multiple_of(near * rows, 8), rows)]
    finish(fetch([(mine, ask), (mine, lows)], out_sems))
    total = out.shape[0] // BATCH
    size = out.shape[0] // groups

    def spot(g):
        peer, inside = divmod(g * BATCH, size)
        return peer * (rows // groups) + inside // width, inside % width

    def copy_in(g):
        line, first = spot(g)

        def one(i, carry):
            tile = jnp.maximum(ask[line, first + i], 0) // TILE
            pltpu.make_async_copy(book_ref.at[tile], land.at[g * BATCH + i], sems.at[g]).start()
            return carry

        lax.fori_loop(0, BATCH, one, 0, unroll=16)

    for g in range(total):
        pl.when(ask[spot(g)] >= 0)(functools.partial(copy_in, g))
    low = jnp.concatenate([(lows[...] % TILE).astype(F32), jnp.zeros((width - rows, width), F32)], axis=0).T
    at = lax.broadcasted_iota(jnp.int32, (BATCH, BATCH * TILE), 1)
    at = at - TILE * lax.broadcasted_iota(jnp.int32, (BATCH, BATCH * TILE), 0)
    at = at.astype(F32)
    for g in range(total):
        span = slice(g * BATCH, (g + 1) * BATCH)
        line, first = spot(g)
        filled = ask[line, first] >= 0

        @pl.when(filled)
        def _(g=g, span=span, line=line, first=first):
            block = land.at[pl.ds(g * BATCH, BATCH)]
            pltpu.make_async_copy(book_ref.at[pl.ds(0, BATCH)], block, sems.at[g]).wait()
            tiles = land[span].reshape(BATCH * TILE, land.shape[-1])
            wanted = onehot(at == low[first : first + BATCH, line : line + 1])
            out[span, :] = jnp.dot(wanted, tiles, preferred_element_type=F32).astype(BF16)

        @pl.when(jnp.logical_not(filled))
        def _(span=span):
            out[span, :] = jnp.zeros((BATCH, out.shape[-1]), BF16)

    parts = []
    for k in range(groups):
        peer = lax.rem(here + k, groups)
        parts.append((out.at[pl.ds(pl.multiple_of(peer * size, BATCH), size)], outs[k]))
    finish(fetch(parts, out_sems))


def join_kernel(before, own, _, _asked, top, bottom, held, sems):
    frames, rows = own.shape[:2]
    old, new = pl.ds(0, frames), pl.ds(frames, frames)
    first, last = pl.ds(0, 1), pl.ds(rows - 1, 1)
    ins = fetch(
        [
            (before.at[:, first], held.at[0, old]),
            (own.at[:, first], held.at[0, new]),
            (before.at[:, last], held.at[1, old]),
            (own.at[:, last], held.at[1, new]),
        ],
        sems,
    )
    finish(ins[2:])
    outs = fetch([(held.at[1], bottom)], sems.at[pl.ds(4, 1)])
    finish(ins[:2])
    outs += fetch([(held.at[0], top)], sems.at[pl.ds(5, 1)])
    finish(outs)


def taps(patch, weight, columns):
    flat = patch.shape[0]
    place = lax.broadcasted_iota(jnp.int32, (flat, 1), 0) % columns
    sums = [jnp.dot(patch, weight(r), preferred_element_type=F32) for r in range(3)]
    left = jnp.where(place == 0, 0.0, pltpu.roll(sums[0], 1, 0))
    right = jnp.where(place == columns - 1, 0.0, pltpu.roll(sums[2], flat - 1, 0))
    return sums[1] + left + right


def frame_taps(window, weight, frame, count, t):
    rows, columns, channels = window.shape[1] - 2, window.shape[2], window.shape[3]
    pieces = [
        window[frame : frame + count, q : q + rows].reshape(count * rows * columns, channels) for q in range(3)
    ]
    return taps(
        jnp.concatenate(pieces, axis=1), lambda r: weight[t, :, r].reshape(3 * channels, channels), columns
    ).reshape(count, rows, columns, channels)


def edge_taps(window, weight, side):
    columns, channels = window.shape[2], window.shape[3]
    row, q = (0, 0) if side == 0 else (window.shape[1] - 1, 2)
    one, two = window[2, row], window[3, row]
    before = jnp.concatenate([jnp.zeros_like(one), one], axis=0)
    patch = jnp.concatenate([before, jnp.concatenate([one, two], axis=0)], axis=1)
    return taps(
        patch, lambda r: weight[1:, q, r].reshape(2 * channels, channels), columns
    ).reshape(2, 1, columns, channels)


def own_kernel(change, own, residual, weight, _, partial, done, window, source, result, sems):
    frames, rows, columns, channels = source.shape
    copies = fetch([(own, window.at[pl.ds(2, frames), pl.ds(1, rows)]), (residual, source)], sems)
    empty = jnp.zeros((frames, 1, columns, channels), BF16)
    window[2:, 0:1] = empty
    window[2:, rows + 1 :] = empty
    done[...] = jnp.zeros_like(done)
    copies[0].wait()
    if change:
        for f in range(2, frames + 2):
            window[f, 1 : rows + 1] = act(window[f, 1 : rows + 1].astype(F32)).astype(BF16)
    copies[1].wait()
    result[...] = source[...].astype(F32) + frame_taps(window, weight, 2, 2, 2)
    first = fetch([(result.at[0], partial.at[0])], sems.at[pl.ds(2, 1)])
    result[1] += frame_taps(window, weight, 2, 1, 1)[0]
    finish(first + fetch([(result.at[1], partial.at[1])], sems.at[pl.ds(3, 1)]))


def rest(change, before, up, down, partial, weight, window, total, sems):
    frames, rows, columns, channels = total.shape
    copies = fetch(
        [
            (before, window.at[pl.ds(0, 2), pl.ds(1, rows)]),
            (up, window.at[:, pl.ds(0, 1)]),
            (down, window.at[:, pl.ds(rows + 1, 1)]),
            (partial, total),
        ],
        sems,
    )
    finish(copies[:3])
    if change:
        for f in range(frames + 2):
            for span in (slice(0, rows + 2),) if f < 2 else (slice(0, 1), slice(rows + 1, rows + 2)):
                window[f, span] = act(window[f, span].astype(F32)).astype(BF16)
    copies[3].wait()
    total[...] += frame_taps(window, weight, 0, 2, 0)
    total[0:1] += frame_taps(window, weight, 1, 1, 1)
    total[:, 0:1] += edge_taps(window, weight, 0)
    total[:, -1:] += edge_taps(window, weight, 1)


def first_kernel(before, up, down, partial, weight, first, active, done, window, total, a, b, sems):
    done[...] = jnp.zeros_like(done)
    rest(True, before, up, down, partial, weight, window, total, sems)
    outs = []
    for f in range(total.shape[0]):
        a[f] = total[f].astype(BF16)
        b[f] = act(a[f].astype(F32)).astype(BF16)
        for i, (src, dst) in enumerate(((b, active), (a, first))):
            outs.append(pltpu.make_async_copy(src.at[f], dst.at[f], sems.at[4 + 2 * f + i]))
            outs[-1].start()
    finish(outs)


def second_kernel(before, up, down, partial, weight, place, encoded, terms, window, total, a, packed, sems):
    rest(False, before, up, down, partial, weight, window, total, sems)
    frames, rows, columns, channels = total.shape
    a[...] = total[...].astype(BF16)
    outs = fetch([(a, encoded)], sems.at[pl.ds(4, 1)])
    flat = a[...].reshape(frames * rows * columns, channels)
    cells = flat.shape[0]
    step = 256
    for i in range(packed.shape[0] // step):
        mine = lax.broadcasted_iota(jnp.int32, (step, cells), 0).astype(F32) + float(i * step) == place[0:1, :]
        span = pl.ds(i * step, step)
        packed[span, :] = jnp.dot(onehot(mine), flat, preferred_element_type=F32).astype(BF16)
        outs.append(pltpu.make_async_copy(packed.at[span], terms.at[span], sems.at[5 + i]))
        outs[-1].start()
    finish(outs)


def rotate_kernel(place, encoded, upstream, *refs):
    found, (grad, rows_in, e_in, g_in, out, sems) = refs[:-6], refs[-6:]
    size = found[0].shape[0]
    parts = [(part, rows_in.at[pl.ds(k * size, size)]) for k, part in enumerate(found)]
    copies = fetch([(encoded, e_in), (upstream, g_in)] + parts, sems)
    cells, slots = out.shape[0], rows_in.shape[0]
    column = place[...].T[:, 1:2]
    finish(copies)
    step = 256
    for i in range(cells // step):
        span = slice(i * step, (i + 1) * step)
        mine = onehot(lax.broadcasted_iota(jnp.int32, (step, slots), 1).astype(F32) == column[span])
        q = jnp.dot(mine, rows_in[...], preferred_element_type=F32)
        e = e_in[span, :].astype(F32)
        g = g_in[span, :].astype(F32)
        lat_norm = jnp.sqrt(jnp.sum(e * e, -1, keepdims=True) + 1e-06)
        quant_norm = jnp.sqrt(jnp.sum(q * q, -1, keepdims=True) + 1e-06)
        a = e / lat_norm
        b = q / quant_norm
        cosine = jnp.sum(a * b, -1, keepdims=True)
        s = a + b
        turned = g - s * (jnp.sum(s * g, -1, keepdims=True) / (1.0 + cosine))
        turned = turned + 2.0 * a * jnp.sum(b * g, -1, keepdims=True)
        out[span, :] = (quant_norm / lat_norm * turned + 2.0 * COMMIT * (e - q)).astype(BF16)
    finish(fetch([(out, grad)], sems.at[pl.ds(0, 1)]))


def sort_kernel(capacity, codes_ref, bounds_ref, order_ref, sorted_ref, named_ref):
    sources = codes_ref.shape[0]
    slots = sources * capacity
    blocks = bounds_ref.shape[0]
    chunks = slots // BLOCK
    width = codes_ref.shape[2]
    code = jnp.concatenate([codes_ref[i, 7:8, :capacity] for i in range(sources)], axis=1)
    earlier = onehot(
        lax.broadcasted_iota(jnp.int32, (width, width), 0) < lax.broadcasted_iota(jnp.int32, (width, width), 1)
    )
    block = jnp.where(code >= 0, code // BLOCK, -1)
    hits = jnp.where(lax.broadcasted_iota(jnp.int32, (blocks, slots), 0) == block, 1.0, 0.0)
    before = jnp.zeros((blocks, 1), F32)
    parts = []
    for i in range(slots // width):
        part = hits[:, i * width : (i + 1) * width]
        parts.append(jnp.dot(part.astype(BF16), earlier, preferred_element_type=F32) + before)
        before = before + jnp.sum(part, 1, keepdims=True)
    ranks = jnp.concatenate(parts, axis=1)
    counts = lax.dot_general(jnp.ones((8, slots), BF16), hits.astype(BF16), NT, preferred_element_type=F32)[0:1]
    lower = lax.broadcasted_iota(jnp.int32, (blocks, blocks), 1) < lax.broadcasted_iota(jnp.int32, (blocks, blocks), 0)
    starts = jnp.sum(jnp.where(lower, counts, 0.0), 1, keepdims=True)
    lane = lax.broadcasted_iota(jnp.int32, (blocks, width), 1)
    bounds_ref[...] = jnp.where(lane == 0, starts, starts + before).astype(jnp.int32)
    order = jnp.sum(hits * (ranks + starts), 0, keepdims=True)
    order = jnp.where(code >= 0, order, -1.0)
    order_ref[...] = order
    at = order.astype(jnp.int32)
    chunk = lax.broadcasted_iota(jnp.int32, (chunks, slots), 0) == jnp.where(at >= 0, at // BLOCK, -1)
    ones = jnp.where(chunk, 1.0, 0.0)
    picked = jnp.concatenate(
        [ones * (code // BLOCK).astype(F32), ones * (code % BLOCK).astype(F32), ones], axis=0
    ).astype(BF16)
    chosen = onehot(lax.broadcasted_iota(jnp.int32, (BLOCK, slots), 0) == at % BLOCK)
    spread = lax.dot_general(picked, chosen, NT, preferred_element_type=F32)
    inside = jnp.where(
        spread[2 * chunks :] > 0.5, spread[:chunks] * float(BLOCK) + spread[chunks : 2 * chunks], -1.0
    )
    sorted_ref[...] = jnp.full(sorted_ref.shape, -1, jnp.int32)
    sorted_ref[:chunks, :] = inside.astype(jnp.int32)
    low = onehot(lax.broadcasted_iota(jnp.int32, (BLOCK, slots), 0) == jnp.where(code >= 0, code % BLOCK, -1))
    named = lax.dot_general(low, hits.astype(BF16), NT, preferred_element_type=F32)
    named_ref[...] = jnp.zeros(named_ref.shape, F32)
    named_ref[:, :blocks] = named


def scatter_kernel(here, bounds, terms, book, order, codes, named, grad, rows_in, book_in, ranked, out, sums, sems):
    slots = rows_in.shape[0]
    chunks = slots // BLOCK
    blocks = out.shape[0] // BLOCK
    own = pl.ds(pl.multiple_of(here[0] * out.shape[0], BLOCK), out.shape[0])
    copies = fetch([(terms, rows_in), (book.at[own], book_in)], sems)
    copies[0].wait()
    at_slot = lax.broadcasted_iota(jnp.int32, (BLOCK, slots), 0).astype(F32)

    def rank(i, carry):
        mine = onehot(at_slot == order[...] - (i * BLOCK).astype(F32))
        span = pl.ds(pl.multiple_of(i * BLOCK, BLOCK), BLOCK)
        ranked[span, :] = jnp.dot(mine, rows_in[...], preferred_element_type=F32).astype(BF16)
        return carry

    lax.fori_loop(0, chunks, rank, 0)
    ranked[slots:, :] = jnp.zeros((ranked.shape[0] - slots, ranked.shape[1]), BF16)
    copies[1].wait()
    at_row = lax.broadcasted_iota(jnp.int32, (BLOCK, BLOCK), 0)
    step = 8

    def part(b, j):
        mine = onehot(at_row == codes[pl.ds(j, 1), :] - b * BLOCK)
        rows = ranked[pl.ds(pl.multiple_of(j * BLOCK, BLOCK), BLOCK), :]
        return jnp.dot(mine, rows, preferred_element_type=F32)

    def leave(b):
        span = pl.ds(pl.multiple_of(b * BLOCK, BLOCK), BLOCK)
        return pltpu.make_async_copy(out.at[span], grad.at[span], sems.at[2 + b])

    def several(g, carry):
        counts = pltpu.roll(named[...], lax.rem(named.shape[1] - g * step, named.shape[1]), 1)
        for i in range(step):
            b = g * step + i
            first = bounds[b, 0] // BLOCK
            span = pl.ds(pl.multiple_of(b * BLOCK, BLOCK), BLOCK)
            total = part(b, first) + part(b, first + 1)
            out[span, :] = (2.0 * (counts[:, i : i + 1] * book_in[span, :].astype(F32) - total)).astype(BF16)
            leave(b).start()
        return carry

    lax.fori_loop(0, blocks // step, several, 0)

    def last(b, carry):
        first = bounds[b, 0] // BLOCK
        after = (bounds[b, 1] + BLOCK - 1) // BLOCK
        leave(b).wait()

        @pl.when(after > first + 2)
        def _():
            span = pl.ds(pl.multiple_of(b * BLOCK, BLOCK), BLOCK)
            sums[...] = jnp.zeros_like(sums)

            def more(j, carry):
                sums[...] += part(b, j)
                return carry

            lax.fori_loop(first, after, more, 0)
            counts = pltpu.roll(named[...], lax.rem(named.shape[1] - b, named.shape[1]), 1)
            out[span, :] = (2.0 * (counts[:, 0:1] * book_in[span, :].astype(F32) - sums[...])).astype(BF16)
            leave(b).start()
            leave(b).wait()

        return carry

    lax.fori_loop(0, blocks, last, 0)


def shape(dims, dtype=BF16):
    return jax.ShapeDtypeStruct(tuple(dims), dtype)


def halo(video, done, asked):
    before = along(video, "tm", 1)
    frames, _, columns, channels = video.shape
    both = shape((2 * frames, 1, columns, channels))
    top, bottom = pl.pallas_call(
        join_kernel,
        out_shape=(both, both),
        in_specs=[HBM, HBM, VMEM, HBM],
        out_specs=(HBM,) * 2,
        scratch_shapes=[pltpu.VMEM((2,) + both.shape, BF16), pltpu.SemaphoreType.DMA((6,))],
        compiler_params=params(8),
    )(before, video, done, asked)
    return before, along(bottom, "height", 1), along(top, "height", -1)


def on_device(latents, conv_first, conv_second, codebook, codes, upstream):
    frames, rows, columns, channels = latents.shape
    cells = frames * rows * columns
    held = codebook.shape[0]
    tiles = lax.axis_size("tm")
    groups = lax.axis_size("height")
    owners = tiles * groups
    range_rows = held // tiles
    capacity = 2 * cells // owners
    slots = owners * capacity
    block = (frames, rows, columns, channels)
    window = pltpu.VMEM((frames + 2, rows + 2, columns, channels), BF16)
    token = shape((8, 128), F32)
    sems = pltpu.SemaphoreType.DMA
    here = jnp.stack([lax.axis_index("tm").astype(jnp.int32), lax.axis_index("height").astype(jnp.int32)])

    def alone(change, own, residual, weight, after):
        return pl.pallas_call(
            functools.partial(own_kernel, change),
            out_shape=(shape(block, F32), token),
            in_specs=[HBM, HBM, VMEM, VMEM],
            out_specs=(HBM, VMEM),
            scratch_shapes=[window, pltpu.VMEM(block, BF16), pltpu.VMEM(block, F32), sems((4,))],
            compiler_params=params(),
        )(own, residual, weight, after)

    send, place = pl.pallas_call(
        functools.partial(index_kernel, groups, tiles, held, capacity),
        out_shape=(shape((owners, 8, columns), jnp.int32), shape((8, cells), F32)),
        in_specs=[SMEM, VMEM],
        out_specs=(VMEM,) * 2,
        compiler_params=params(),
    )(here, codes.reshape(frames * rows, columns))
    asked = lax.all_to_all(send, ("tm", "height"), split_axis=0, concat_axis=0, tiled=True)
    partial, done = alone(True, latents, latents, conv_first, place)
    before, up, down = halo(latents, done, asked)
    first, active, done = pl.pallas_call(
        first_kernel,
        out_shape=(shape(block), shape(block), token),
        in_specs=[HBM] * 4 + [VMEM],
        out_specs=(HBM, HBM, VMEM),
        scratch_shapes=[
            window,
            pltpu.VMEM(block, F32),
            pltpu.VMEM(block, BF16),
            pltpu.VMEM(block, BF16),
            sems((4 + 2 * frames,)),
        ],
        compiler_params=params(),
    )(before, up, down, partial, conv_first)

    *found, done = pl.pallas_call(
        functools.partial(gather_kernel, groups),
        out_shape=(shape((slots // groups, channels)),) * groups + (token,),
        in_specs=[SMEM, HBM, HBM, VMEM],
        out_specs=(HBM,) * groups + (VMEM,),
        scratch_shapes=[
            pltpu.SMEM((groups * 8, columns), jnp.int32),
            pltpu.VMEM((groups * 8, columns), jnp.int32),
            pltpu.VMEM((slots, TILE, channels), BF16),
            pltpu.VMEM((slots, channels), BF16),
            sems((slots // BATCH,)),
            sems((groups,)),
        ],
        compiler_params=params(),
    )(here, asked.reshape(owners * 8, columns), codebook.reshape(held // TILE, TILE, channels), done)
    partial, done = alone(False, active, first, conv_second, done)
    before, up, down = halo(active, done, done)
    encoded, terms = pl.pallas_call(
        second_kernel,
        out_shape=(shape(block), shape((slots, channels))),
        in_specs=[HBM] * 4 + [VMEM] * 2,
        out_specs=(HBM,) * 2,
        scratch_shapes=[
            window,
            pltpu.VMEM(block, F32),
            pltpu.VMEM(block, BF16),
            pltpu.VMEM((slots, channels), BF16),
            sems((5 + slots // 256,)),
        ],
        compiler_params=params(),
    )(before, up, down, partial, conv_second, place)

    owner_terms = lax.all_to_all(
        terms.reshape(owners, capacity, channels), ("tm", "height"), split_axis=0, concat_axis=0, tiled=True
    )
    found = [found[0]] + [around(found[k], "height", k) for k in range(1, groups)]
    blocks = range_rows // BLOCK
    chunks = slots // BLOCK
    bounds, order, ranked, named = pl.pallas_call(
        functools.partial(sort_kernel, capacity),
        out_shape=(
            shape((blocks, 128), jnp.int32),
            shape((1, slots), F32),
            shape((-(-(chunks + 2) // 8) * 8, BLOCK), jnp.int32),
            shape((BLOCK, 128), F32),
        ),
        in_specs=[VMEM],
        out_specs=(VMEM,) * 4,
        compiler_params=params(),
    )(asked)
    grad = pl.pallas_call(
        rotate_kernel,
        out_shape=shape((cells, channels)),
        in_specs=[VMEM] + [HBM] * (2 + groups),
        out_specs=HBM,
        scratch_shapes=[pltpu.VMEM((slots, channels), BF16)] + [pltpu.VMEM((cells, channels), BF16)] * 3
        + [sems((2 + groups,))],
        compiler_params=params(),
    )(
        place,
        encoded.reshape(cells, channels),
        upstream.reshape(cells, channels),
        *found,
    )
    codebook_grad = pl.pallas_call(
        scatter_kernel,
        out_shape=shape((range_rows, channels)),
        in_specs=[SMEM, SMEM, HBM, HBM, VMEM, VMEM, VMEM],
        out_specs=HBM,
        scratch_shapes=[
            pltpu.VMEM((slots, channels), BF16),
            pltpu.VMEM((range_rows, channels), BF16),
            pltpu.VMEM((slots + 2 * BLOCK, channels), BF16),
            pltpu.VMEM((range_rows, channels), BF16),
            pltpu.VMEM((BLOCK, channels), F32),
            sems((2 + blocks,)),
        ],
        compiler_params=params(),
    )(here, bounds, owner_terms.reshape(slots, channels), codebook, order, ranked, named)
    return (grad.reshape(upstream.shape), codebook_grad)


def solution(mesh):
    return jax.shard_map(
        on_device,
        mesh=mesh,
        in_specs=(
            P("tm", "height", None, None),
            P(),
            P(),
            P("height", None),
            P("tm", "height", None),
            P("tm", "height", None, None),
        ),
        out_specs=(P("tm", "height", None, None), P(("height", "tm"), None)),
        check_vma=False,
    )
```

profile of v0, /device:TPU:1, one launch (start us, length us, event | category | flops | bytes accessed | tf_op | source)
XLA Modules:
  0.0 118.7 jit_solution(9729934533243638410)
XLA Ops:
  0.6 4.8 %collective-permute-start = (bf16[2,4,128,256]{3,2,1,0:T(8,128)(2,1)}, bf16[2,4,128,256]{3,2,1,0:T(8,128)(2,1)}, u32[]{:S(2)}, u32[]{:S(2)}) collective-permute-start(bf16[2,4,128,256]{3,2,1,0:T(8,128)(2,1)} %own.3), channel_id=1, source_target_pairs={{0,4},{4,8},{8,12},{12,16},{16,20},{20,24},{24,28},{1,5},{5,9},{9,... | collective-permute-start | bytes 1572872 | tf_op jit(solution)/shard_map/ppermute | solution.py:24
  5.5 0.7 copy-done.11
  6.2 2.0 %shard_map.77 = (s32[32,8,128]{2,1,0:T(8,128)}, f32[8,1024]{1,0:T(8,128)S(1)}) custom-call(s32[2]{0:T(128)S(1)} %pad_add_fusion.here_ref.here, s32[8,128]{1,0:T(8,128)S(1)} %bitcast.13), custom_call_target="tpu_custom_call" | custom-call | tf_op jit(solution)/shard_map/pallas_call | solution.py:477
  8.8 4.9 %all-to-all-start = ((s32[32,8,128]{2,1,0:T(8,128)}), s32[32,8,128]{2,1,0:T(8,128)}, u32[]{:S(2)}, u32[]{:S(2)}) async-start(s32[32,8,128]{2,1,0:T(8,128)} %get-tuple-element.28), calls=%async_computation | async-start | bytes 262144 | tf_op jit(solution)/shard_map/all_to_all | solution.py:484
  13.6 2.0 %copy-done = bf16[3,3,3,256,256]{4,3,2,1,0:T(8,128)(2,1)S(1)} copy-done((bf16[3,3,3,256,256]{4,3,2,1,0:T(8,128)(2,1)S(1)}, bf16[3,3,3,256,256]{4,3,2,1,0:T(8,128)(2,1)}, u32[]{:S(2)}) %copy-start) | copy-done | bytes 3538968
  15.6 1.0 copy-done.3
  16.7 0.8 copy-done.9
  17.4 3.2 %shard_map.78 = (f32[2,4,128,256]{3,2,1,0:T(8,128)S(1)}, f32[8,128]{1,0:T(8,128)S(1)}) custom-call(bf16[2,4,128,256]{3,2,1,0:T(8,128)(2,1)S(1)} %copy-done.3, bf16[2,4,128,256]{3,2,1,0:T(8,128)(2,1)S(1)} %copy-done.3, bf16[3,3,3,256,256]{4,3,2,1,0:T(8,128)(2,1)S(1)} %copy-done, f32[8,1024]{1,0:T(8,128)S(1)} %copy-done.9), custom_call_target="tpu_custom_call" | custom-call | tf_op jit(solution)/shard_map/pallas_call | solution.py:468
  20.7 1.0 copy-done.5
  21.9 1.0 copy-done.4
  22.9 1.1 shard_map.79
  24.0 3.3 %collective-permute-start.1 = (bf16[4,1,128,256]{3,2,1,0:T(8,128)(2,1)S(1)}, bf16[4,1,128,256]{3,2,1,0:T(8,128)(2,1)S(1)}, u32[]{:S(2)}, u32[]{:S(2)}) collective-permute-start(bf16[4,1,128,256]{3,2,1,0:T(8,128)(2,1)S(1)} %get-tuple-element.29), channel_id=1, source_target_pairs={{0,1},{1,2},{2,3},{4,5},{5,6},{6,7},{8,9},{9,10},{10,11},{12,13},{... | collective-permute-start | bytes 786440 | tf_op jit(solution)/shard_map/ppermute | solution.py:24
  27.4 1.9 %collective-permute-start.2 = (bf16[4,1,128,256]{3,2,1,0:T(8,128)(2,1)S(1)}, bf16[4,1,128,256]{3,2,1,0:T(8,128)(2,1)S(1)}, u32[]{:S(2)}, u32[]{:S(2)}) collective-permute-start(bf16[4,1,128,256]{3,2,1,0:T(8,128)(2,1)S(1)} %get-tuple-element.30), channel_id=1, source_target_pairs={{1,0},{2,1},{3,2},{5,4},{6,5},{7,6},{9,8},{10,9},{11,10},{13,12},{... | collective-permute-start | bytes 786440 | tf_op jit(solution)/shard_map/ppermute | solution.py:24
  29.3 1.4 %collective-permute-done.1.up = bf16[4,1,128,256]{3,2,1,0:T(8,128)(2,1)S(1)} collective-permute-done((bf16[4,1,128,256]{3,2,1,0:T(8,128)(2,1)S(1)}, bf16[4,1,128,256]{3,2,1,0:T(8,128)(2,1)S(1)}, u32[]{:S(2)}, u32[]{:S(2)}) %collective-permute-start.1) | collective-permute-done | bytes 262176 | tf_op jit(solution)/shard_map/ppermute | solution.py:24
  30.6 4.4 %collective-permute-done.2.down = bf16[4,1,128,256]{3,2,1,0:T(8,128)(2,1)S(1)} collective-permute-done((bf16[4,1,128,256]{3,2,1,0:T(8,128)(2,1)S(1)}, bf16[4,1,128,256]{3,2,1,0:T(8,128)(2,1)S(1)}, u32[]{:S(2)}, u32[]{:S(2)}) %collective-permute-start.2) | collective-permute-done | bytes 262176 | tf_op jit(solution)/shard_map/ppermute | solution.py:24
  35.0 1.2 %copy-done.6 = f32[2,4,128,256]{3,2,1,0:T(8,128)S(1)} copy-done((f32[2,4,128,256]{3,2,1,0:T(8,128)S(1)}, f32[2,4,128,256]{3,2,1,0:T(8,128)}, u32[]{:S(2)}) %copy-start.6) | copy-done | bytes 1048600
  36.3 4.8 %shard_map.80 = (bf16[2,4,128,256]{3,2,1,0:T(8,128)(2,1)S(1)}, bf16[2,4,128,256]{3,2,1,0:T(8,128)(2,1)S(1)}, f32[8,128]{1,0:T(8,128)S(1)}) custom-call(bf16[2,4,128,256]{3,2,1,0:T(8,128)(2,1)} %collective-permute-done.before, bf16[4,1,128,256]{3,2,1,0:T(8,128)(2,1)S(1)} %collective-permute-done.1.up, ...), custom_call_target="tpu_custom_call" | custom-call | tf_op jit(solution)/shard_map/pallas_call | solution.py:487
  41.1 3.1 %collective-permute-start.3 = (bf16[2,4,128,256]{3,2,1,0:T(8,128)(2,1)S(1)}, bf16[2,4,128,256]{3,2,1,0:T(8,128)(2,1)S(1)}, u32[]{:S(2)}, u32[]{:S(2)}) collective-permute-start(bf16[2,4,128,256]{3,2,1,0:T(8,128)(2,1)S(1)} %get-tuple-element.32.own), channel_id=1, source_target_pairs={{0,4},{4,8},{8,12},{12,16},{16,20},{20,24},{24,28},{1,5},{5,9},{9,... | collective-permute-start | bytes 1572872 | tf_op jit(solution)/shard_map/ppermute | solution.py:24
  44.3 15.6 %shard_map.81 = (bf16[512,256]{1,0:T(8,128)(2,1)S(1)}, bf16[512,256]{1,0:T(8,128)(2,1)S(1)}, bf16[512,256]{1,0:T(8,128)(2,1)S(1)}, bf16[512,256]{1,0:T(8,128)(2,1)S(1)}, f32[8,128]{1,0:T(8,128)S(1)}) custom-call(s32[2]{0:T(128)S(1)} %pad_add_fusion.here_ref.here, s32[256,128]{1,0:T(8,128)} %bitcast.3.asked_ref, bf16[4096,16,256]{2,1,0:T(8,128)(2,1)} %bitcast.14, ...), custom_call_target="tpu_custom_call" | custom-call | tf_op jit(solution)/shard_map/pallas_call | solution.py:502
  59.9 2.8 %shard_map.82 = (f32[2,4,128,256]{3,2,1,0:T(8,128)S(1)}, f32[8,128]{1,0:T(8,128)S(1)}) custom-call(bf16[2,4,128,256]{3,2,1,0:T(8,128)(2,1)S(1)} %get-tuple-element.32.own, bf16[2,4,128,256]{3,2,1,0:T(8,128)(2,1)S(1)} %get-tuple-element.33.residual, bf16[3,3,3,256,256]{4,3,2,1,0:T(8,128)(2,1)S(1)} %copy-done.2, f32[8,128]{1,0:T(8,128)S(1)} %get-tuple-element.35._), custom_call_target="tpu_custom_call" | custom-call | tf_op jit(solution)/shard_map/pallas_call | solution.py:468
  63.2 2.1 %collective-permute-start.4 = (bf16[4,1,128,256]{3,2,1,0:T(8,128)(2,1)S(1)}, bf16[4,1,128,256]{3,2,1,0:T(8,128)(2,1)S(1)}, u32[]{:S(2)}, u32[]{:S(2)}) collective-permute-start(bf16[4,1,128,256]{3,2,1,0:T(8,128)(2,1)S(1)} %get-tuple-element.37), channel_id=1, source_target_pairs={{0,1},{1,2},{2,3},{4,5},{5,6},{6,7},{8,9},{9,10},{10,11},{12,13},{... | collective-permute-start | bytes 786440 | tf_op jit(solution)/shard_map/ppermute | solution.py:24
  65.2 2.4 %collective-permute-start.5 = (bf16[4,1,128,256]{3,2,1,0:T(8,128)(2,1)S(1)}, bf16[4,1,128,256]{3,2,1,0:T(8,128)(2,1)S(1)}, u32[]{:S(2)}, u32[]{:S(2)}) collective-permute-start(bf16[4,1,128,256]{3,2,1,0:T(8,128)(2,1)S(1)} %get-tuple-element.38), channel_id=1, source_target_pairs={{1,0},{2,1},{3,2},{5,4},{6,5},{7,6},{9,8},{10,9},{11,10},{13,12},{... | collective-permute-start | bytes 786440 | tf_op jit(solution)/shard_map/ppermute | solution.py:24
  67.7 0.9 collective-permute-done.4.up
  68.5 4.4 %collective-permute-done.5.down = bf16[4,1,128,256]{3,2,1,0:T(8,128)(2,1)S(1)} collective-permute-done((bf16[4,1,128,256]{3,2,1,0:T(8,128)(2,1)S(1)}, bf16[4,1,128,256]{3,2,1,0:T(8,128)(2,1)S(1)}, u32[]{:S(2)}, u32[]{:S(2)}) %collective-permute-start.5) | collective-permute-done | bytes 262176 | tf_op jit(solution)/shard_map/ppermute | solution.py:24
  72.9 4.7 %shard_map.84 = (bf16[2,4,128,256]{3,2,1,0:T(8,128)(2,1)S(1)}, bf16[2048,256]{1,0:T(8,128)(2,1)}) custom-call(bf16[2,4,128,256]{3,2,1,0:T(8,128)(2,1)S(1)} %collective-permute-done.3.before, bf16[4,1,128,256]{3,2,1,0:T(8,128)(2,1)S(1)} %collective-permute-done.4.up, bf16[4,1,128,256]{3,2,1,0:T(8,128)(2,1)S(1)} %collective-permute-done.5.down, ...), custom_call_target="tpu_custom_call" | custom-call | tf_op jit(solution)/shard_map/pallas_call | solution.py:519
  77.6 3.6 %all-to-all-start.1 = ((bf16[32,64,256]{2,1,0:T(8,128)(2,1)}), bf16[32,64,256]{2,1,0:T(8,128)(2,1)S(1)}, u32[]{:S(2)}, u32[]{:S(2)}) async-start(bf16[32,64,256]{2,1,0:T(8,128)(2,1)} %bitcast.8), calls=%async_computation.1 | async-start | bytes 2097152 | tf_op jit(solution)/shard_map/all_to_all | solution.py:534
  81.2 1.7 %collective-permute-start.6 = (bf16[512,256]{1,0:T(8,128)(2,1)S(1)}, bf16[512,256]{1,0:T(8,128)(2,1)S(1)}, u32[]{:S(2)}, u32[]{:S(2)}) collective-permute-start(bf16[512,256]{1,0:T(8,128)(2,1)S(1)} %get-tuple-element.42), channel_id=1, source_target_pairs={{0,1},{1,2},{2,3},{3,0},{4,5},{5,6},{6,7},{7,4},{8,9},{9,10},{10,1... | collective-permute-start | bytes 786440 | tf_op jit(solution)/shard_map/ppermute | solution.py:29
  83.4 2.1 %shard_map.86 = (s32[32,128]{1,0:T(8,128)S(1)}, f32[1,2048]{1,0:T(1,128)S(1)}, s32[16,256]{1,0:T(8,128)S(1)}, f32[256,128]{1,0:T(8,128)S(1)}) custom-call(s32[32,8,128]{2,1,0:T(8,128)} %all-to-all-done._asked.codes_ref), custom_call_target="tpu_custom_call" | custom-call | tf_op jit(solution)/shard_map/pallas_call | solution.py:540
  85.6 10.2 %collective-permute-done.6.refs_1_ = bf16[512,256]{1,0:T(8,128)(2,1)S(1)} collective-permute-done((bf16[512,256]{1,0:T(8,128)(2,1)S(1)}, bf16[512,256]{1,0:T(8,128)(2,1)S(1)}, u32[]{:S(2)}, u32[]{:S(2)}) %collective-permute-start.6) | collective-permute-done | bytes 262176 | tf_op jit(solution)/shard_map/ppermute | solution.py:29
  95.7 9.8 %collective-permute-done.7.refs_2_ = bf16[512,256]{1,0:T(8,128)(2,1)S(1)} collective-permute-done((bf16[512,256]{1,0:T(8,128)(2,1)S(1)}, bf16[512,256]{1,0:T(8,128)(2,1)S(1)}, u32[]{:S(2)}, u32[]{:S(2)}) %collective-permute-start.7) | collective-permute-done | bytes 262176 | tf_op jit(solution)/shard_map/ppermute | solution.py:29
  106.1 3.4 %shard_map.85 = bf16[1024,256]{1,0:T(8,128)(2,1)} custom-call(f32[8,1024]{1,0:T(8,128)S(1)} %copy-done.10, bf16[1024,256]{1,0:T(8,128)(2,1)S(1)} %bitcast.12, bf16[1024,256]{1,0:T(8,128)(2,1)S(1)} %bitcast.11, bf16[512,256]{1,0:T(8,128)(2,1)S(1)} %get-tuple-element.41.refs_0_, bf16[512,256]{1,0:T(8,128)(2,1)S(1)} %collective-permute-done.6.refs_1_, ...), custom_call_target="tpu_custom_call" | custom-call | tf_op jit(solution)/shard_map/pallas_call | solution.py:552
  109.5 9.0 %shard_map.87 = bf16[8192,256]{1,0:T(8,128)(2,1)} custom-call(s32[2]{0:T(128)S(1)} %pad_add_fusion.here_ref.here, s32[32,128]{1,0:T(8,128)S(1)} %get-tuple-element.45.bounds, bf16[2048,256]{1,0:T(8,128)(2,1)S(1)} %bitcast.10, bf16[65536,256]{1,0:T(8,128)(2,1)} %book.1, f32[1,2048]{1,0:T(1,128)S(1)} %get-tuple-element.47.order, ...), custom_call_target="tpu_custom_call" | custom-call | tf_op jit(solution)/shard_map/pallas_call | solution.py:566
  (26 shorter events, 2.5 us)
Async XLA Ops:
  0.6 21.3 %collective-permute-start = (bf16[2,4,128,256]{3,2,1,0:T(8,128)(2,1)}, bf16[2,4,128,256]{3,2,1,0:T(8,128)(2,1)}, u32[]{:S(2)}, u32[]{:S(2)}) collective-permute-start(bf16[2,4,128,256]{3,2,1,0:T(8,128)(2,1)} %own.3), channel_id=1, source_target_pairs={{0,4},{4,8},{8,12},{12,16},{16,20},{20,24},{24,28},{1,5},{5,9},{9,... | collective-permute-start | bytes 1572872 | tf_op jit(solution)/shard_map/ppermute | solution.py:24
  5.5 0.7 copy-start.11
  8.2 0.6 copy-start.8
  8.8 13.1 %all-to-all-start = ((s32[32,8,128]{2,1,0:T(8,128)}), s32[32,8,128]{2,1,0:T(8,128)}, u32[]{:S(2)}, u32[]{:S(2)}) async-start(s32[32,8,128]{2,1,0:T(8,128)} %get-tuple-element.28), calls=%async_computation | async-start | bytes 262144 | tf_op jit(solution)/shard_map/all_to_all | solution.py:484
  13.6 2.0 %copy-start = (bf16[3,3,3,256,256]{4,3,2,1,0:T(8,128)(2,1)S(1)}, bf16[3,3,3,256,256]{4,3,2,1,0:T(8,128)(2,1)}, u32[]{:S(2)}) copy-start(bf16[3,3,3,256,256]{4,3,2,1,0:T(8,128)(2,1)} %weight.5) | copy-start | bytes 10616836
  15.6 1.0 copy-start.3
  16.7 0.8 copy-start.9
  17.4 17.6 %copy-start.1 = (bf16[3,3,3,256,256]{4,3,2,1,0:T(8,128)(2,1)S(1)}, bf16[3,3,3,256,256]{4,3,2,1,0:T(8,128)(2,1)}, u32[]{:S(2)}) copy-start(bf16[3,3,3,256,256]{4,3,2,1,0:T(8,128)(2,1)} %weight.5) | copy-start | bytes 10616836
  20.7 1.0 copy-start.5
  21.9 1.0 copy-start.4
  24.0 6.6 %collective-permute-start.1 = (bf16[4,1,128,256]{3,2,1,0:T(8,128)(2,1)S(1)}, bf16[4,1,128,256]{3,2,1,0:T(8,128)(2,1)S(1)}, u32[]{:S(2)}, u32[]{:S(2)}) collective-permute-start(bf16[4,1,128,256]{3,2,1,0:T(8,128)(2,1)S(1)} %get-tuple-element.29), channel_id=1, source_target_pairs={{0,1},{1,2},{2,3},{4,5},{5,6},{6,7},{8,9},{9,10},{10,11},{12,13},{... | collective-permute-start | bytes 786440 | tf_op jit(solution)/shard_map/ppermute | solution.py:24
  27.4 7.7 %collective-permute-start.2 = (bf16[4,1,128,256]{3,2,1,0:T(8,128)(2,1)S(1)}, bf16[4,1,128,256]{3,2,1,0:T(8,128)(2,1)S(1)}, u32[]{:S(2)}, u32[]{:S(2)}) collective-permute-start(bf16[4,1,128,256]{3,2,1,0:T(8,128)(2,1)S(1)} %get-tuple-element.30), channel_id=1, source_target_pairs={{1,0},{2,1},{3,2},{5,4},{6,5},{7,6},{9,8},{10,9},{11,10},{13,12},{... | collective-permute-start | bytes 786440 | tf_op jit(solution)/shard_map/ppermute | solution.py:24
  35.0 1.2 %copy-start.6 = (f32[2,4,128,256]{3,2,1,0:T(8,128)S(1)}, f32[2,4,128,256]{3,2,1,0:T(8,128)}, u32[]{:S(2)}) copy-start(f32[2,4,128,256]{3,2,1,0:T(8,128)} %copy-done.5) | copy-start | bytes 3145732
  41.1 21.6 %collective-permute-start.3 = (bf16[2,4,128,256]{3,2,1,0:T(8,128)(2,1)S(1)}, bf16[2,4,128,256]{3,2,1,0:T(8,128)(2,1)S(1)}, u32[]{:S(2)}, u32[]{:S(2)}) collective-permute-start(bf16[2,4,128,256]{3,2,1,0:T(8,128)(2,1)S(1)} %get-tuple-element.32.own), channel_id=1, source_target_pairs={{0,4},{4,8},{8,12},{12,16},{16,20},{20,24},{24,28},{1,5},{5,9},{9,... | collective-permute-start | bytes 1572872 | tf_op jit(solution)/shard_map/ppermute | solution.py:24
  44.3 15.7 %copy-start.2 = (bf16[3,3,3,256,256]{4,3,2,1,0:T(8,128)(2,1)S(1)}, bf16[3,3,3,256,256]{4,3,2,1,0:T(8,128)(2,1)}, u32[]{:S(2)}) copy-start(bf16[3,3,3,256,256]{4,3,2,1,0:T(8,128)(2,1)} %weight.7) | copy-start | bytes 10616836
  59.9 13.0 %copy-start.10 = (f32[8,1024]{1,0:T(8,128)S(1)}, f32[8,1024]{1,0:T(8,128)}, u32[]{:S(2)}) copy-start(f32[8,1024]{1,0:T(8,128)} %copy-done.8) | copy-start | bytes 98308
  63.2 42.9 %copy-start.7 = (bf16[2,4,128,256]{3,2,1,0:T(8,128)(2,1)S(1)}, bf16[2,4,128,256]{3,2,1,0:T(8,128)(2,1)}, u32[]{:S(2)}) copy-start(bf16[2,4,128,256]{3,2,1,0:T(8,128)(2,1)} %param.11) | copy-start | bytes 1572868
  63.2 5.4 %collective-permute-start.4 = (bf16[4,1,128,256]{3,2,1,0:T(8,128)(2,1)S(1)}, bf16[4,1,128,256]{3,2,1,0:T(8,128)(2,1)S(1)}, u32[]{:S(2)}, u32[]{:S(2)}) collective-permute-start(bf16[4,1,128,256]{3,2,1,0:T(8,128)(2,1)S(1)} %get-tuple-element.37), channel_id=1, source_target_pairs={{0,1},{1,2},{2,3},{4,5},{5,6},{6,7},{8,9},{9,10},{10,11},{12,13},{... | collective-permute-start | bytes 786440 | tf_op jit(solution)/shard_map/ppermute | solution.py:24
  65.2 7.7 %collective-permute-start.5 = (bf16[4,1,128,256]{3,2,1,0:T(8,128)(2,1)S(1)}, bf16[4,1,128,256]{3,2,1,0:T(8,128)(2,1)S(1)}, u32[]{:S(2)}, u32[]{:S(2)}) collective-permute-start(bf16[4,1,128,256]{3,2,1,0:T(8,128)(2,1)S(1)} %get-tuple-element.38), channel_id=1, source_target_pairs={{1,0},{2,1},{3,2},{5,4},{6,5},{7,6},{9,8},{10,9},{11,10},{13,12},{... | collective-permute-start | bytes 786440 | tf_op jit(solution)/shard_map/ppermute | solution.py:24
  77.6 31.8 %all-to-all-start.1 = ((bf16[32,64,256]{2,1,0:T(8,128)(2,1)}), bf16[32,64,256]{2,1,0:T(8,128)(2,1)S(1)}, u32[]{:S(2)}, u32[]{:S(2)}) async-start(bf16[32,64,256]{2,1,0:T(8,128)(2,1)} %bitcast.8), calls=%async_computation.1 | async-start | bytes 2097152 | tf_op jit(solution)/shard_map/all_to_all | solution.py:534
  81.2 14.5 %collective-permute-start.6 = (bf16[512,256]{1,0:T(8,128)(2,1)S(1)}, bf16[512,256]{1,0:T(8,128)(2,1)S(1)}, u32[]{:S(2)}, u32[]{:S(2)}) collective-permute-start(bf16[512,256]{1,0:T(8,128)(2,1)S(1)} %get-tuple-element.42), channel_id=1, source_target_pairs={{0,1},{1,2},{2,3},{3,0},{4,5},{5,6},{6,7},{7,4},{8,9},{9,10},{10,1... | collective-permute-start | bytes 786440 | tf_op jit(solution)/shard_map/ppermute | solution.py:29
  82.9 22.6 %collective-permute-start.7 = (bf16[512,256]{1,0:T(8,128)(2,1)S(1)}, bf16[512,256]{1,0:T(8,128)(2,1)S(1)}, u32[]{:S(2)}, u32[]{:S(2)}) collective-permute-start(bf16[512,256]{1,0:T(8,128)(2,1)S(1)} %get-tuple-element.43), channel_id=1, source_target_pairs={{0,2},{1,3},{2,0},{3,1},{4,6},{5,7},{6,4},{7,5},{8,10},{9,11},{10,... | collective-permute-start | bytes 786440 | tf_op jit(solution)/shard_map/ppermute | solution.py:29
  82.9 23.2 %collective-permute-start.8 = (bf16[512,256]{1,0:T(8,128)(2,1)S(1)}, bf16[512,256]{1,0:T(8,128)(2,1)S(1)}, u32[]{:S(2)}, u32[]{:S(2)}) collective-permute-start(bf16[512,256]{1,0:T(8,128)(2,1)S(1)} %get-tuple-element.44), channel_id=1, source_target_pairs={{0,3},{1,0},{2,1},{3,2},{4,7},{5,4},{6,5},{7,6},{8,11},{9,8},{10,9... | collective-permute-start | bytes 786440 | tf_op jit(solution)/shard_map/ppermute | solution.py:29
where the time goes:
time: 119 us
  Pallas kernels  49.2 us (41%)
  waiting for transfers between devices  31.8 us (27%)
  starting transfers between devices  28.3 us (24%)
  local copies, waits for them, and re-layouts  8.34 us (7%)
    ppermute x3, waiting for transfers between devices, around(): return lax.ppermute(x, axis, [(i, (i + by) % count) for i in range(count)])  20.5 us
    ppermute x6, starting transfers between devices, along(): lax.ppermute(x, axis, [(i, i + by) for i in range(count) if 0 <= i + by <...  17.6 us
    pallas_call x1, Pallas kernels, on_device(): pl.pallas_call(functools.partial(gather_kernel, groups), out_shape=(shape...  15.6 us
    ppermute x6, waiting for transfers between devices, along(): lax.ppermute(x, axis, [(i, i + by) for i in range(count) if 0 <= i + by <...  11 us
    pallas_call x1, Pallas kernels, on_device(): pl.pallas_call(scatter_kernel, out_shape=shape((range_rows, channels)), i...  9.01 us
    unnamed x24, local copies, waits for them, and re-layouts  8.34 us
    pallas_call x2, Pallas kernels, alone(): pl.pallas_call(functools.partial(own_kernel, change), out_shape=(shape(bl...  6.03 us
    all_to_all x1, starting transfers between devices, on_device(): lax.all_to_all(send, ('tm', 'height'), split_axis=0, concat_axis=0, tiled...  4.87 us
  transfers between devices with their start and end apart: 11, of which 8 were waited for; matrix products, arithmetic and copies ran while one was open for 0% of the time, Pallas kernels for 25%

commit v1 on v0

--- a/solution.py
+++ b/solution.py
@@ -58,116 +58,121 @@
     return jnp.where(mask, 1.0, 0.0).astype(BF16)
 
 
-def index_kernel(groups, tiles, held, capacity, here_ref, codes_ref, send_ref, place_ref):
-    lines, width = codes_ref.shape
+def index_kernel(groups, tiles, held, capacity, where_ref, codes_ref, ask_ref, low_ref, place_ref):
+    lines, width = codes_ref.shape[1:]
     cells = lines * width
     owners = groups * tiles
     range_rows = held // tiles
     block_slots = tiles * capacity
-    near, here = here_ref[0], here_ref[1]
-    own = lanes(codes_ref[...])
+    batches = block_slots // BATCH
+    here = where_ref[0]
+    own = lanes(codes_ref[here])
     block = own // range_rows
     target = block % tiles * groups + block // tiles
     home = own // held
+    arrival = lax.rem(here - home + groups, groups)
+    peers = [lanes(codes_ref[lax.rem(here + k, groups)]) for k in range(groups)]
     own_hits = lax.broadcasted_iota(jnp.int32, (owners, cells), 0) == target
-    home_hits = lax.broadcasted_iota(jnp.int32, (groups, cells), 0) == home
-    pad = -(owners + groups) % 16
+    home_hits = lax.broadcasted_iota(jnp.int32, (groups, cells), 0) == arrival
+    peer_hits = [peer // held == here for peer in peers]
     hits = jnp.concatenate(
-        [jnp.where(own_hits, 1.0, 0.0), jnp.where(home_hits, 1.0, 0.0), jnp.zeros((pad, cells), F32)], axis=0
-    )
+        [jnp.where(own_hits, 1.0, 0.0), jnp.where(home_hits, 1.0, 0.0)] + [jnp.where(x, 1.0, 0.0) for x in peer_hits], axis=0
+    )
+    count = hits.shape[0]
+    pad = -count % 16
+    if pad:
+        hits = jnp.concatenate([hits, jnp.zeros((pad, cells), F32)], axis=0)
     earlier = onehot(
         lax.broadcasted_iota(jnp.int32, (width, width), 0) < lax.broadcasted_iota(jnp.int32, (width, width), 1)
     )
-    before = jnp.zeros((hits.shape[0], 1), F32)
+    before = jnp.zeros((count + pad, 1), F32)
     parts = []
     for i in range(lines):
         part = hits[:, i * width : (i + 1) * width]
         parts.append(jnp.dot(part.astype(BF16), earlier, preferred_element_type=F32) + before)
         before = before + jnp.sum(part, 1, keepdims=True)
-    ranks = hits * jnp.concatenate(parts, axis=1)
-    own_rank = jnp.sum(ranks[:owners], 0, keepdims=True)
-    home_rank = jnp.sum(ranks[owners : owners + groups], 0, keepdims=True)
-    arrival = lax.rem(here - home + groups, groups)
+    ranks = jnp.concatenate(parts, axis=1)
+    own_rank = jnp.sum(ranks[:owners] * hits[:owners], 0, keepdims=True)
+    home_rank = jnp.sum(ranks[owners : owners + groups] * hits[owners : owners + groups], 0, keepdims=True)
     place_ref[0:1, :] = target.astype(F32) * capacity + own_rank
     place_ref[1:2, :] = arrival.astype(F32) * block_slots + home_rank
     place_ref[2:, :] = jnp.zeros((6, cells), F32)
-    send_ref[...] = jnp.zeros(send_ref.shape, jnp.int32)
-
-    def spread(ones, code, rank):
-        count = ones.shape[0]
-        high, low = (code // 256).astype(F32), (code % 256).astype(F32)
-        picked = jnp.concatenate([ones * high, ones * low, ones], axis=0).astype(BF16)
-        chosen = onehot(lax.broadcasted_iota(jnp.int32, (width, cells), 0) == rank)
-        out = lax.dot_general(picked, chosen, NT, preferred_element_type=F32)
-        code = out[:count] * 256.0 + out[count : 2 * count]
-        return jnp.where(out[2 * count :] > 0.5, code, -1.0).astype(jnp.int32)
-
-    send_ref[:, 7, :] = spread(hits[:owners], own % range_rows, own_rank.astype(jnp.int32))
-    asked_lines = block_slots // width
-    line = home_rank.astype(jnp.int32) // width
-    for h in range(groups):
-        ones = jnp.where(
-            (lax.broadcasted_iota(jnp.int32, (8, cells), 0) == line) & (home == h), 1.0, 0.0
-        )
-        asked = spread(ones, own % held, home_rank.astype(jnp.int32) % width)
-        send_ref[near * groups + h, 0:asked_lines, :] = asked[:asked_lines]
-
-
-def gather_kernel(groups, here_ref, asked_ref, book_ref, _, *refs):
-    outs, (done, ask, lows, land, out, sems, out_sems) = refs[:groups], refs[groups:]
+    columns = []
+    for k in range(groups):
+        hit = hits[owners + groups + k : owners + groups + k + 1]
+        rank = ranks[owners + groups + k : owners + groups + k + 1].astype(jnp.int32)
+        row = jnp.where(peer_hits[k], peers[k] - here * held, 0)
+        batch = onehot(
+            lax.broadcasted_iota(jnp.int32, (batches, cells), 0) == jnp.where(peer_hits[k], rank // BATCH, -1)
+        ).astype(F32)
+        tile = row // TILE
+        picked = jnp.concatenate(
+            [
+                batch * (tile // 128).astype(F32),
+                batch * (tile % 128).astype(F32),
+                batch,
+                batch * (row % TILE).astype(F32),
+            ],
+            axis=0,
+        ).astype(BF16)
+        chosen = onehot(lax.broadcasted_iota(jnp.int32, (BATCH, cells), 0) == rank % BATCH)
+        slots = lax.dot_general(picked, chosen, NT, preferred_element_type=F32)
+        asked = slots[:batches] * 128.0 + slots[batches : 2 * batches]
+        ask_ref[k * batches : (k + 1) * batches, :] = jnp.where(
+            slots[2 * batches : 3 * batches] > 0.5, asked, -1.0
+        ).astype(jnp.int32)
+        columns.append(lax.dot_general(chosen, picked[3 * batches :], NT, preferred_element_type=F32))
+    low_ref[...] = jnp.concatenate(columns, axis=1)
+
+
+def gather_kernel(which, ask_ref, book_ref, low_ref, _, *refs):
+    groups = len(which)
+    outs, (done, land, out, sems, out_sems) = refs[:groups], refs[groups:]
     done[...] = jnp.zeros_like(done)
-    rows, width = ask.shape
-    near, here = here_ref[0], here_ref[1]
-    mine = asked_ref.at[pl.ds(pl.multiple_of(near * rows, 8), rows)]
-    finish(fetch([(mine, ask), (mine, lows)], out_sems))
     total = out.shape[0] // BATCH
-    size = out.shape[0] // groups
-
-    def spot(g):
-        peer, inside = divmod(g * BATCH, size)
-        return peer * (rows // groups) + inside // width, inside % width
+    skip = which[0] * (total // groups)
 
     def copy_in(g):
-        line, first = spot(g)
-
         def one(i, carry):
-            tile = jnp.maximum(ask[line, first + i], 0) // TILE
+            tile = jnp.maximum(ask_ref[skip + g, i], 0)
             pltpu.make_async_copy(book_ref.at[tile], land.at[g * BATCH + i], sems.at[g]).start()
             return carry
 
         lax.fori_loop(0, BATCH, one, 0, unroll=16)
 
     for g in range(total):
-        pl.when(ask[spot(g)] >= 0)(functools.partial(copy_in, g))
-    low = jnp.concatenate([(lows[...] % TILE).astype(F32), jnp.zeros((width - rows, width), F32)], axis=0).T
+        pl.when(ask_ref[skip + g, 0] >= 0)(functools.partial(copy_in, g))
     at = lax.broadcasted_iota(jnp.int32, (BATCH, BATCH * TILE), 1)
     at = at - TILE * lax.broadcasted_iota(jnp.int32, (BATCH, BATCH * TILE), 0)
     at = at.astype(F32)
     for g in range(total):
         span = slice(g * BATCH, (g + 1) * BATCH)
-        line, first = spot(g)
-        filled = ask[line, first] >= 0
+        filled = ask_ref[skip + g, 0] >= 0
 
         @pl.when(filled)
-        def _(g=g, span=span, line=line, first=first):
+        def _(g=g, span=span):
             block = land.at[pl.ds(g * BATCH, BATCH)]
             pltpu.make_async_copy(book_ref.at[pl.ds(0, BATCH)], block, sems.at[g]).wait()
             tiles = land[span].reshape(BATCH * TILE, land.shape[-1])
-            wanted = onehot(at == low[first : first + BATCH, line : line + 1])
-            out[span, :] = jnp.dot(wanted, tiles, preferred_element_type=F32).astype(BF16)
+            out[span, :] = jnp.dot(onehot(at == low_ref[:, skip + g : skip + g + 1]), tiles, preferred_element_type=F32).astype(BF16)
 
         @pl.when(jnp.logical_not(filled))
         def _(span=span):
             out[span, :] = jnp.zeros((BATCH, out.shape[-1]), BF16)
 
-    parts = []
-    for k in range(groups):
-        peer = lax.rem(here + k, groups)
-        parts.append((out.at[pl.ds(pl.multiple_of(peer * size, BATCH), size)], outs[k]))
-    finish(fetch(parts, out_sems))
-
-
-def join_kernel(before, own, _, _asked, top, bottom, held, sems):
+    size = out.shape[0] // groups
+    finish(fetch([(out.at[pl.ds(k * size, size)], outs[k]) for k in range(groups)], out_sems))
+
+
+def double(own, other, both):
+    count = own.shape[0]
+    both[:count] = own[...]
+    both[count:] = other[...]
+
+
+def join_kernel(before, own, _, codes, others, top, bottom, codes_out, done, held, sems):
+    done[...] = jnp.zeros_like(done)
+    double(codes, others, codes_out)
     frames, rows = own.shape[:2]
     old, new = pl.ds(0, frames), pl.ds(frames, frames)
     first, last = pl.ds(0, 1), pl.ds(rows - 1, 1)
@@ -196,14 +201,12 @@
     return sums[1] + left + right
 
 
-def frame_taps(window, weight, frame, count, t):
+def frame_taps(window, weight, frame, count):
     rows, columns, channels = window.shape[1] - 2, window.shape[2], window.shape[3]
     pieces = [
         window[frame : frame + count, q : q + rows].reshape(count * rows * columns, channels) for q in range(3)
     ]
-    return taps(
-        jnp.concatenate(pieces, axis=1), lambda r: weight[t, :, r].reshape(3 * channels, channels), columns
-    ).reshape(count, rows, columns, channels)
+    return taps(jnp.concatenate(pieces, axis=1), weight, columns).reshape(count, rows, columns, channels)
 
 
 def edge_taps(window, weight, side):
@@ -217,9 +220,18 @@
     ).reshape(2, 1, columns, channels)
 
 
-def own_kernel(change, own, residual, weight, _, partial, done, window, source, result, sems):
+def own_kernel(change, own, residual, weight, *refs):
+    partial, done, window, source, taken, result, sems = refs[-7:]
     frames, rows, columns, channels = source.shape
-    copies = fetch([(own, window.at[pl.ds(2, frames), pl.ds(1, rows)]), (residual, source)], sems)
+    copies = fetch(
+        [
+            (own, window.at[pl.ds(2, frames), pl.ds(1, rows)]),
+            (weight.at[2], taken.at[1]),
+            (residual, source),
+            (weight.at[1], taken.at[0]),
+        ],
+        sems,
+    )
     empty = jnp.zeros((frames, 1, columns, channels), BF16)
     window[2:, 0:1] = empty
     window[2:, rows + 1 :] = empty
@@ -228,10 +240,30 @@
     if change:
         for f in range(2, frames + 2):
             window[f, 1 : rows + 1] = act(window[f, 1 : rows + 1].astype(F32)).astype(BF16)
-    copies[1].wait()
-    result[...] = source[...].astype(F32) + frame_taps(window, weight, 2, 2, 2)
+    finish(copies[1:3])
+    wide = 3 * channels
+    result[...] = source[...].astype(F32) + frame_taps(
+        window, lambda r: taken[1, :, r].reshape(wide, channels), 2, 2
+    )
+    first = fetch([(result.at[0], partial.at[0])], sems.at[pl.ds(4, 1)])
+    copies[3].wait()
+    result[1] += frame_taps(window, lambda r: taken[0, :, r].reshape(wide, channels), 2, 1)[0]
+    finish(first + fetch([(result.at[1], partial.at[1])], sems.at[pl.ds(5, 1)]))
+
+
+def own_second_kernel(own, residual, weight, _, partial, window, source, result, sems):
+    frames, rows, columns, channels = source.shape
+    copies = fetch([(own, window.at[pl.ds(2, frames), pl.ds(1, rows)]), (residual, source)], sems)
+    empty = jnp.zeros((frames, 1, columns, channels), BF16)
+    window[2:, 0:1] = empty
+    window[2:, rows + 1 :] = empty
+    finish(copies)
+    wide = 3 * channels
+    result[...] = source[...].astype(F32) + frame_taps(
+        window, lambda r: weight[2, :, r].reshape(wide, channels), 2, 2
+    )
     first = fetch([(result.at[0], partial.at[0])], sems.at[pl.ds(2, 1)])
-    result[1] += frame_taps(window, weight, 2, 1, 1)[0]
+    result[1] += frame_taps(window, lambda r: weight[1, :, r].reshape(wide, channels), 2, 1)[0]
     finish(first + fetch([(result.at[1], partial.at[1])], sems.at[pl.ds(3, 1)]))
 
 
@@ -252,14 +284,18 @@
             for span in (slice(0, rows + 2),) if f < 2 else (slice(0, 1), slice(rows + 1, rows + 2)):
                 window[f, span] = act(window[f, span].astype(F32)).astype(BF16)
     copies[3].wait()
-    total[...] += frame_taps(window, weight, 0, 2, 0)
-    total[0:1] += frame_taps(window, weight, 1, 1, 1)
+    wide = 3 * channels
+    total[...] += frame_taps(window, lambda r: weight[0, :, r].reshape(wide, channels), 0, 2)
+    total[0:1] += frame_taps(window, lambda r: weight[1, :, r].reshape(wide, channels), 1, 1)
     total[:, 0:1] += edge_taps(window, weight, 0)
     total[:, -1:] += edge_taps(window, weight, 1)
 
 
-def first_kernel(before, up, down, partial, weight, first, active, done, window, total, a, b, sems):
+def first_kernel(
+    before, up, down, partial, weight, codes, others, first, active, codes_out, done, window, total, a, b, sems
+):
     done[...] = jnp.zeros_like(done)
+    double(codes, others, codes_out)
     rest(True, before, up, down, partial, weight, window, total, sems)
     outs = []
     for f in range(total.shape[0]):
@@ -271,7 +307,10 @@
     finish(outs)
 
 
-def second_kernel(before, up, down, partial, weight, place, encoded, terms, window, total, a, packed, sems):
+def second_kernel(before, up, down, partial, weight, place, codes, others, *refs):
+    encoded, terms, codes_out, done, window, total, a, packed, sems = refs
+    done[...] = jnp.zeros_like(done)
+    double(codes, others, codes_out)
     rest(False, before, up, down, partial, weight, window, total, sems)
     frames, rows, columns, channels = total.shape
     a[...] = total[...].astype(BF16)
@@ -315,16 +354,46 @@
     finish(fetch([(out, grad)], sems.at[pl.ds(0, 1)]))
 
 
-def sort_kernel(capacity, codes_ref, bounds_ref, order_ref, sorted_ref, named_ref):
-    sources = codes_ref.shape[0]
+def sort_kernel(tiles, capacity, near, here, every, bounds_ref, order_ref, sorted_ref, named_ref, codes_ref):
+    groups = every.shape[0] // tiles
+    for k in range(tiles):
+        codes_ref[pl.ds((near[0] ^ k) * groups, groups)] = every[k * groups : (k + 1) * groups]
+    sources, lines, width = codes_ref.shape
+    rows = bounds_ref.shape[0] * BLOCK
+    mine = (here[0] * tiles + near[0]) * rows
+    cells = lines * width
     slots = sources * capacity
     blocks = bounds_ref.shape[0]
     chunks = slots // BLOCK
-    width = codes_ref.shape[2]
-    code = jnp.concatenate([codes_ref[i, 7:8, :capacity] for i in range(sources)], axis=1)
     earlier = onehot(
         lax.broadcasted_iota(jnp.int32, (width, width), 0) < lax.broadcasted_iota(jnp.int32, (width, width), 1)
     )
+    parts, ranks = [], []
+    before = jnp.zeros((sources, 1), F32)
+    for i in range(lines):
+        local = codes_ref[:, i, :] - mine
+        inside = (local >= 0) & (local < rows)
+        part = jnp.where(inside, 1.0, 0.0)
+        rank = jnp.dot(part.astype(BF16), earlier, preferred_element_type=F32) + before
+        before = before + jnp.sum(part, 1, keepdims=True)
+        parts.append(jnp.where(inside, local, -1))
+        ranks.append(jnp.where(inside, rank, -1.0))
+    parts, ranks = jnp.concatenate(parts, axis=1), jnp.concatenate(ranks, axis=1)
+    picked_high = jnp.where(parts >= 0, parts // 256, 0).astype(F32)
+    picked_low = jnp.where(parts >= 0, parts % 256, 0).astype(F32)
+    picked_one = jnp.where(parts >= 0, 1.0, 0.0)
+    slot = lax.broadcasted_iota(jnp.int32, (capacity, cells), 0).astype(F32)
+    found = []
+    for i in range(sources):
+        span = slice(i, i + 1)
+        picked = jnp.concatenate(
+            [picked_high[span], picked_low[span], picked_one[span], jnp.zeros((5, cells), F32)], axis=0
+        )
+        found.append(
+            lax.dot_general(picked.astype(BF16), onehot(slot == ranks[span]), NT, preferred_element_type=F32)
+        )
+    found = jnp.concatenate(found, axis=1)
+    code = jnp.where(found[2:3] > 0.5, found[0:1] * 256.0 + found[1:2], -1.0).astype(jnp.int32)
     block = jnp.where(code >= 0, code // BLOCK, -1)
     hits = jnp.where(lax.broadcasted_iota(jnp.int32, (blocks, slots), 0) == block, 1.0, 0.0)
     before = jnp.zeros((blocks, 1), F32)
@@ -433,19 +502,25 @@
     return jax.ShapeDtypeStruct(tuple(dims), dtype)
 
 
-def halo(video, done, asked):
+def halo(video, after, codes, others):
     before = along(video, "tm", 1)
     frames, _, columns, channels = video.shape
     both = shape((2 * frames, 1, columns, channels))
-    top, bottom = pl.pallas_call(
+    more = shape((2 * codes.shape[0],) + codes.shape[1:], jnp.int32)
+    top, bottom, codes, done = pl.pallas_call(
         join_kernel,
-        out_shape=(both, both),
-        in_specs=[HBM, HBM, VMEM, HBM],
-        out_specs=(HBM,) * 2,
+        out_shape=(both, both, more, shape((8, 128), F32)),
+        in_specs=[HBM] * 2 + [VMEM] * 3,
+        out_specs=(HBM, HBM, VMEM, VMEM),
         scratch_shapes=[pltpu.VMEM((2,) + both.shape, BF16), pltpu.SemaphoreType.DMA((6,))],
-        compiler_params=params(8),
-    )(before, video, done, asked)
-    return before, along(bottom, "height", 1), along(top, "height", -1)
+        compiler_params=params(),
+    )(before, video, after, codes, others)
+    return before, along(bottom, "height", 1), along(top, "height", -1), codes, done
+
+
+def swapped(codes, axis, by):
+    count = lax.axis_size(axis)
+    return lax.ppermute(codes, axis, [(i, i ^ by) for i in range(count)])
 
 
 def on_device(latents, conv_first, conv_second, codebook, codes, upstream):
@@ -460,95 +535,107 @@
     slots = owners * capacity
     block = (frames, rows, columns, channels)
     window = pltpu.VMEM((frames + 2, rows + 2, columns, channels), BF16)
+    whole = pltpu.VMEM(block, F32)
+    half = pltpu.VMEM(block, BF16)
     token = shape((8, 128), F32)
     sems = pltpu.SemaphoreType.DMA
-    here = jnp.stack([lax.axis_index("tm").astype(jnp.int32), lax.axis_index("height").astype(jnp.int32)])
-
-    def alone(change, own, residual, weight, after):
+    near = lax.axis_index("tm").astype(jnp.int32).reshape(1)
+    here = lax.axis_index("height").astype(jnp.int32).reshape(1)
+
+    def code_lines(count):
+        return shape((count * groups, frames * rows, columns), jnp.int32)
+
+    shared = lax.all_gather(codes.reshape(frames * rows, columns), "height")
+    ask, low, place = pl.pallas_call(
+        functools.partial(index_kernel, groups, tiles, held, capacity),
+        out_shape=(
+            shape((slots // BATCH, BATCH), jnp.int32),
+            shape((BATCH, slots // BATCH), F32),
+            shape((8, cells), F32),
+        ),
+        in_specs=[SMEM, VMEM],
+        out_specs=(VMEM,) * 3,
+        compiler_params=params(),
+    )(here, shared)
+    every = shared
+    by = 1
+    while by * 8 < tiles:
+        every = jnp.concatenate([every, swapped(every, "tm", by)])
+        by *= 2
+    partial, done = pl.pallas_call(
+        functools.partial(own_kernel, True),
+        out_shape=(shape(block, F32), token),
+        in_specs=[HBM] * 4,
+        out_specs=(HBM, VMEM),
+        scratch_shapes=[window, half, pltpu.VMEM((2, 3, 3, channels, channels), BF16), whole, sems((6,))],
+        compiler_params=params(28),
+    )(latents, latents, conv_first, place)
+    before, up, down, _, done = halo(latents, done, shared, shared)
+    first, active, every, done = pl.pallas_call(
+        first_kernel,
+        out_shape=(shape(block), shape(block), code_lines(2 * by), token),
+        in_specs=[HBM] * 4 + [VMEM] * 3,
+        out_specs=(HBM, HBM, VMEM, VMEM),
+        scratch_shapes=[window, whole, half, half, sems((4 + 2 * frames,))],
+        compiler_params=params(),
+    )(before, up, down, partial, conv_first, every, swapped(every, "tm", by))
+    by *= 2
+
+    def lookup(which, after):
         return pl.pallas_call(
-            functools.partial(own_kernel, change),
-            out_shape=(shape(block, F32), token),
-            in_specs=[HBM, HBM, VMEM, VMEM],
-            out_specs=(HBM, VMEM),
-            scratch_shapes=[window, pltpu.VMEM(block, BF16), pltpu.VMEM(block, F32), sems((4,))],
+            functools.partial(gather_kernel, which),
+            out_shape=(shape((slots // groups, channels)),) * len(which) + (token,),
+            in_specs=[SMEM, HBM, VMEM, VMEM],
+            out_specs=(HBM,) * len(which) + (VMEM,),
+            scratch_shapes=[
+                pltpu.VMEM((slots // groups * len(which), TILE, channels), BF16),
+                pltpu.VMEM((slots // groups * len(which), channels), BF16),
+                sems((slots // groups * len(which) // BATCH,)),
+                sems((len(which),)),
+            ],
             compiler_params=params(),
-        )(own, residual, weight, after)
-
-    send, place = pl.pallas_call(
-        functools.partial(index_kernel, groups, tiles, held, capacity),
-        out_shape=(shape((owners, 8, columns), jnp.int32), shape((8, cells), F32)),
-        in_specs=[SMEM, VMEM],
-        out_specs=(VMEM,) * 2,
-        compiler_params=params(),
-    )(here, codes.reshape(frames * rows, columns))
-    asked = lax.all_to_all(send, ("tm", "height"), split_axis=0, concat_axis=0, tiled=True)
-    partial, done = alone(True, latents, latents, conv_first, place)
-    before, up, down = halo(latents, done, asked)
-    first, active, done = pl.pallas_call(
-        first_kernel,
-        out_shape=(shape(block), shape(block), token),
-        in_specs=[HBM] * 4 + [VMEM],
-        out_specs=(HBM, HBM, VMEM),
-        scratch_shapes=[
-            window,
-            pltpu.VMEM(block, F32),
-            pltpu.VMEM(block, BF16),
-            pltpu.VMEM(block, BF16),
-            sems((4 + 2 * frames,)),
-        ],
-        compiler_params=params(),
-    )(before, up, down, partial, conv_first)
-
-    *found, done = pl.pallas_call(
-        functools.partial(gather_kernel, groups),
-        out_shape=(shape((slots // groups, channels)),) * groups + (token,),
-        in_specs=[SMEM, HBM, HBM, VMEM],
-        out_specs=(HBM,) * groups + (VMEM,),
-        scratch_shapes=[
-            pltpu.SMEM((groups * 8, columns), jnp.int32),
-            pltpu.VMEM((groups * 8, columns), jnp.int32),
-            pltpu.VMEM((slots, TILE, channels), BF16),
-            pltpu.VMEM((slots, channels), BF16),
-            sems((slots // BATCH,)),
-            sems((groups,)),
-        ],
-        compiler_params=params(),
-    )(here, asked.reshape(owners * 8, columns), codebook.reshape(held // TILE, TILE, channels), done)
-    partial, done = alone(False, active, first, conv_second, done)
-    before, up, down = halo(active, done, done)
-    encoded, terms = pl.pallas_call(
+        )(ask, codebook.reshape(held // TILE, TILE, channels), low, after)
+
+    *found, done = lookup(range(1, groups), done)
+    before, up, down, every, done = halo(active, done, every, swapped(every, "tm", by))
+    by *= 2
+    partial = pl.pallas_call(
+        own_second_kernel,
+        out_shape=shape(block, F32),
+        in_specs=[HBM] * 2 + [VMEM] * 2,
+        out_specs=HBM,
+        scratch_shapes=[window, half, whole, sems((4,))],
+        compiler_params=params(),
+    )(active, first, conv_second, done)
+    encoded, terms, every, done = pl.pallas_call(
         second_kernel,
-        out_shape=(shape(block), shape((slots, channels))),
-        in_specs=[HBM] * 4 + [VMEM] * 2,
-        out_specs=(HBM,) * 2,
-        scratch_shapes=[
-            window,
-            pltpu.VMEM(block, F32),
-            pltpu.VMEM(block, BF16),
-            pltpu.VMEM((slots, channels), BF16),
-            sems((5 + slots // 256,)),
-        ],
-        compiler_params=params(),
-    )(before, up, down, partial, conv_second, place)
+        out_shape=(shape(block), shape((slots, channels)), code_lines(2 * by), token),
+        in_specs=[HBM] * 4 + [VMEM] * 4,
+        out_specs=(HBM, HBM, VMEM, VMEM),
+        scratch_shapes=[window, whole, half, pltpu.VMEM((slots, channels), BF16), sems((5 + slots // 256,))],
+        compiler_params=params(),
+    )(before, up, down, partial, conv_second, place, every, swapped(every, "tm", by))
 
     owner_terms = lax.all_to_all(
         terms.reshape(owners, capacity, channels), ("tm", "height"), split_axis=0, concat_axis=0, tiled=True
     )
-    found = [found[0]] + [around(found[k], "height", k) for k in range(1, groups)]
+    found = [around(rows_of, "height", k + 1) for k, rows_of in enumerate(found)]
+    found = [lookup(range(1), done)[0]] + found
     blocks = range_rows // BLOCK
     chunks = slots // BLOCK
     bounds, order, ranked, named = pl.pallas_call(
-        functools.partial(sort_kernel, capacity),
+        functools.partial(sort_kernel, tiles, capacity),
         out_shape=(
             shape((blocks, 128), jnp.int32),
             shape((1, slots), F32),
             shape((-(-(chunks + 2) // 8) * 8, BLOCK), jnp.int32),
             shape((BLOCK, 128), F32),
         ),
-        in_specs=[VMEM],
+        in_specs=[SMEM, SMEM, VMEM],
         out_specs=(VMEM,) * 4,
-        compiler_params=params(),
-    )(asked)
+        scratch_shapes=[pltpu.VMEM((owners, frames * rows, columns), jnp.int32)],
+        compiler_params=params(),
+    )(near, here, every)
     grad = pl.pallas_call(
         rotate_kernel,
         out_shape=shape((cells, channels)),
@@ -577,7 +664,7 @@
             sems((2 + blocks,)),
         ],
         compiler_params=params(),
-    )(here, bounds, owner_terms.reshape(slots, channels), codebook, order, ranked, named)
+    )(near, bounds, owner_terms.reshape(slots, channels), codebook, order, ranked, named)
     return (grad.reshape(upstream.shape), codebook_grad)
 
 

time: 119 us -> 107 us (0.90)
  waiting for transfers between devices: 31.8 us -> 20.9 us
  blocking collectives: 0 us -> 6.07 us
  local copies, waits for them, and re-layouts: 8.34 us -> 3.05 us
  Pallas kernels: 49.2 us -> 45.8 us
  starting transfers between devices: 28.3 us -> 29.9 us
    ppermute x6, waiting for transfers between devices: 11 us -> 3.78 us  [along(): lax.ppermute(x, axis, [(i, i + by) for i in range(count) if 0 <= i + by <...]
    all_gather x0 -> x1, blocking collectives: none -> 6.07 us  [on_device(): shared = lax.all_gather(codes.reshape(frames * rows, columns), 'height')]
    ppermute x3, waiting for transfers between devices: 20.5 us -> 14.8 us  [around(): return lax.ppermute(x, axis, [(i, (i + by) % count) for i in range(count)])]
    unnamed x24 -> x12, local copies, waits for them, and re-layouts: 8.34 us -> 3.05 us
    all_to_all x1 -> x0, starting transfers between devices: 4.87 us -> none  [on_device(): lax.all_to_all(send, ('tm', 'height'), split_axis=0, concat_axis=0, tiled...]
    ppermute x0 -> x3, starting transfers between devices: none -> 3.97 us  [swapped(): return lax.ppermute(codes, axis, [(i, i ^ by) for i in range(count)])]
    pallas_call x7 -> x8, Pallas kernels: 30.1 us -> 27.8 us  [the longest x2 12.8 us: lookup(): pl.pallas_call(functools.partial(gather_kernel, which), out_shape=(shape(...]
    ppermute x0 -> x3, waiting for transfers between devices: none -> 2.3 us  [swapped(): return lax.ppermute(codes, axis, [(i, i ^ by) for i in range(count)])]
  transfers between devices with their start and end apart: 11 -> 13, of which waited for: 8 -> 7; matrix products, arithmetic and copies ran while one was open for 0% -> 0% of each run, Pallas kernels for 25% -> 25%
where the time goes in v1:
time: 107 us
  Pallas kernels  45.8 us (43%)
  starting transfers between devices  29.9 us (28%)
  waiting for transfers between devices  20.9 us (20%)
  blocking collectives  6.07 us (6%)
  local copies, waits for them, and re-layouts  3.05 us (3%)
    ppermute x6, starting transfers between devices, along(): lax.ppermute(x, axis, [(i, i + by) for i in range(count) if 0 <= i + by <...  19.3 us
    ppermute x3, waiting for transfers between devices, around(): return lax.ppermute(x, axis, [(i, (i + by) % count) for i in range(count)])  14.8 us
    pallas_call x2, Pallas kernels, lookup(): pl.pallas_call(functools.partial(gather_kernel, which), out_shape=(shape(...  12.8 us
    pallas_call x1, Pallas kernels, on_device(): pl.pallas_call(scatter_kernel, out_shape=shape((range_rows, channels)), i...  9.01 us
    all_gather x1, blocking collectives, on_device(): shared = lax.all_gather(codes.reshape(frames * rows, columns), 'height')  6.07 us
    pallas_call x1, Pallas kernels, on_device(): pl.pallas_call(second_kernel, out_shape=(shape(block), shape((slots, chan...  4.73 us
    all_to_all x1, starting transfers between devices, on_device(): lax.all_to_all(terms.reshape(owners, capacity, channels), ('tm', 'height'...  4.45 us
    pallas_call x1, Pallas kernels, on_device(): pl.pallas_call(first_kernel, out_shape=(shape(block), shape(block), code_...  4 us
  transfers between devices with their start and end apart: 13, of which 7 were waited for; matrix products, arithmetic and copies ran while one was open for 0% of the time, Pallas kernels for 25%

profile of v1, /device:TPU:1, one launch (start us, length us, event | category | flops | bytes accessed | tf_op | source)
XLA Modules:
  0.0 106.8 jit_solution(12125636968925257120)
XLA Ops:
  0.6 4.0 %collective-permute-start = (bf16[2,4,128,256]{3,2,1,0:T(8,128)(2,1)}, bf16[2,4,128,256]{3,2,1,0:T(8,128)(2,1)S(1)}, u32[]{:S(2)}, u32[]{:S(2)}) collective-permute-start(bf16[2,4,128,256]{3,2,1,0:T(8,128)(2,1)} %own.3), channel_id=1, source_target_pairs={{0,4},{4,8},{8,12},{12,16},{16,20},{20,24},{24,28},{1,5},{5,9},{9,... | collective-permute-start | bytes 1572872 | tf_op jit(solution)/shard_map/ppermute | solution.py:24
  4.6 6.1 %all_gather.3.codes_ref.codes.others = s32[4,8,128]{2,1,0:T(8,128)S(1)} all-gather(s32[1,8,128]{2,1,0:T(8,128)} %bitcast.15), channel_id=1, replica_groups=mesh['tm'=8,'height'=4] {'height'}, dimensions={0}, use_global_device_ids=true | all-gather | bytes 20480 | tf_op jit(solution)/shard_map/all_gather | solution.py:548
  10.7 0.9 shard_map.77
  11.7 2.0 %copy-done.1 = bf16[3,3,3,256,256]{4,3,2,1,0:T(8,128)(2,1)S(1)} copy-done((bf16[3,3,3,256,256]{4,3,2,1,0:T(8,128)(2,1)S(1)}, bf16[3,3,3,256,256]{4,3,2,1,0:T(8,128)(2,1)}, u32[]{:S(2)}) %copy-start.1) | copy-done | bytes 3538968
  13.7 1.0 copy-done.3
  14.7 3.7 %shard_map.78 = (f32[2,4,128,256]{3,2,1,0:T(8,128)S(1)}, f32[8,128]{1,0:T(8,128)S(1)}) custom-call(bf16[2,4,128,256]{3,2,1,0:T(8,128)(2,1)S(1)} %copy-done.3, bf16[2,4,128,256]{3,2,1,0:T(8,128)(2,1)S(1)} %copy-done.3, bf16[3,3,3,256,256]{4,3,2,1,0:T(8,128)(2,1)S(1)} %copy-done.1, f32[8,1024]{1,0:T(8,128)S(1)} %get-tuple-element.30.refs_0_.place), custom_call_target="tpu_custom_call" | custom-call | tf_op jit(solution)/shard_map/pallas_call | solution.py:565
  18.5 1.1 shard_map.79
  19.5 3.2 %collective-permute-start.1 = (bf16[4,1,128,256]{3,2,1,0:T(8,128)(2,1)S(1)}, bf16[4,1,128,256]{3,2,1,0:T(8,128)(2,1)S(1)}, u32[]{:S(2)}, u32[]{:S(2)}) collective-permute-start(bf16[4,1,128,256]{3,2,1,0:T(8,128)(2,1)S(1)} %get-tuple-element.32), channel_id=1, source_target_pairs={{0,1},{1,2},{2,3},{4,5},{5,6},{6,7},{8,9},{9,10},{10,11},{12,13},{... | collective-permute-start | bytes 786440 | tf_op jit(solution)/shard_map/ppermute | solution.py:24
  22.8 1.9 %collective-permute-start.2 = (bf16[4,1,128,256]{3,2,1,0:T(8,128)(2,1)S(1)}, bf16[4,1,128,256]{3,2,1,0:T(8,128)(2,1)S(1)}, u32[]{:S(2)}, u32[]{:S(2)}) collective-permute-start(bf16[4,1,128,256]{3,2,1,0:T(8,128)(2,1)S(1)} %get-tuple-element.33), channel_id=1, source_target_pairs={{1,0},{2,1},{3,2},{5,4},{6,5},{7,6},{9,8},{10,9},{11,10},{13,12},{... | collective-permute-start | bytes 786440 | tf_op jit(solution)/shard_map/ppermute | solution.py:24
  24.7 1.3 %collective-permute-start.3 = (s32[4,8,128]{2,1,0:T(8,128)S(1)}, s32[4,8,128]{2,1,0:T(8,128)S(1)}, u32[]{:S(2)}, u32[]{:S(2)}) collective-permute-start(s32[4,8,128]{2,1,0:T(8,128)S(1)} %all_gather.3.codes_ref.codes.others), channel_id=1, source_target_pairs={{0,4},{4,0},{8,12},{12,8},{16,20},{20,16},{24,28},{28,24},{1,5},{5... | collective-permute-start | bytes 49160 | tf_op jit(solution)/shard_map/ppermute | solution.py:523
  26.0 1.4 %collective-permute-done.3.others = s32[4,8,128]{2,1,0:T(8,128)S(1)} collective-permute-done((s32[4,8,128]{2,1,0:T(8,128)S(1)}, s32[4,8,128]{2,1,0:T(8,128)S(1)}, u32[]{:S(2)}, u32[]{:S(2)}) %collective-permute-start.3) | collective-permute-done | bytes 16416 | tf_op jit(solution)/shard_map/ppermute | solution.py:523
  27.3 3.1 %collective-permute-done.2.down = bf16[4,1,128,256]{3,2,1,0:T(8,128)(2,1)S(1)} collective-permute-done((bf16[4,1,128,256]{3,2,1,0:T(8,128)(2,1)S(1)}, bf16[4,1,128,256]{3,2,1,0:T(8,128)(2,1)S(1)}, u32[]{:S(2)}, u32[]{:S(2)}) %collective-permute-start.2) | collective-permute-done | bytes 262176 | tf_op jit(solution)/shard_map/ppermute | solution.py:24
  30.5 4.0 %shard_map.80 = (bf16[2,4,128,256]{3,2,1,0:T(8,128)(2,1)S(1)}, bf16[2,4,128,256]{3,2,1,0:T(8,128)(2,1)S(1)}, s32[8,8,128]{2,1,0:T(8,128)S(1)}, f32[8,128]{1,0:T(8,128)S(1)}) custom-call(bf16[2,4,128,256]{3,2,1,0:T(8,128)(2,1)S(1)} %collective-permute-done.before, bf16[4,1,128,256]{3,2,1,0:T(8,128)(2,1)S(1)} %collective-permute-done.1.up, ...), custom_call_target="tpu_custom_call" | custom-call | tf_op jit(solution)/shard_map/pallas_call | solution.py:574
  34.5 3.1 %collective-permute-start.4 = (bf16[2,4,128,256]{3,2,1,0:T(8,128)(2,1)S(1)}, bf16[2,4,128,256]{3,2,1,0:T(8,128)(2,1)S(1)}, u32[]{:S(2)}, u32[]{:S(2)}) collective-permute-start(bf16[2,4,128,256]{3,2,1,0:T(8,128)(2,1)S(1)} %get-tuple-element.35.own), channel_id=1, source_target_pairs={{0,4},{4,8},{8,12},{12,16},{16,20},{20,24},{24,28},{1,5},{5,9},{9,... | collective-permute-start | bytes 1572872 | tf_op jit(solution)/shard_map/ppermute | solution.py:24
  37.6 1.3 %collective-permute-start.5 = (s32[8,8,128]{2,1,0:T(8,128)S(1)}, s32[8,8,128]{2,1,0:T(8,128)S(1)}, u32[]{:S(2)}, u32[]{:S(2)}) collective-permute-start(s32[8,8,128]{2,1,0:T(8,128)S(1)} %get-tuple-element.40.codes), channel_id=1, source_target_pairs={{0,8},{4,12},{8,0},{12,4},{16,24},{20,28},{24,16},{28,20},{1,9},{5... | collective-permute-start | bytes 98312 | tf_op jit(solution)/shard_map/ppermute | solution.py:523
  39.0 7.9 %shard_map.81 = (bf16[512,256]{1,0:T(8,128)(2,1)S(1)}, bf16[512,256]{1,0:T(8,128)(2,1)S(1)}, bf16[512,256]{1,0:T(8,128)(2,1)S(1)}, f32[8,128]{1,0:T(8,128)S(1)}) custom-call(s32[32,64]{1,0:T(8,128)S(1)} %get-tuple-element.36.ask_ref, bf16[4096,16,256]{2,1,0:T(8,128)(2,1)} %bitcast.12, f32[64,32]{1,0:T(8,128)S(1)} %get-tuple-element.37.low_ref, ...), custom_call_target="tpu_custom_call" | custom-call | tf_op jit(solution)/shard_map/pallas_call | solution.py:585
  47.4 5.1 %collective-permute-start.6 = (bf16[4,1,128,256]{3,2,1,0:T(8,128)(2,1)S(1)}, bf16[4,1,128,256]{3,2,1,0:T(8,128)(2,1)S(1)}, u32[]{:S(2)}, u32[]{:S(2)}) collective-permute-start(bf16[4,1,128,256]{3,2,1,0:T(8,128)(2,1)S(1)} %get-tuple-element.41), channel_id=1, source_target_pairs={{0,1},{1,2},{2,3},{4,5},{5,6},{6,7},{8,9},{9,10},{10,11},{12,13},{... | collective-permute-start | bytes 786440 | tf_op jit(solution)/shard_map/ppermute | solution.py:24
  52.4 1.9 %collective-permute-start.7 = (bf16[4,1,128,256]{3,2,1,0:T(8,128)(2,1)S(1)}, bf16[4,1,128,256]{3,2,1,0:T(8,128)(2,1)S(1)}, u32[]{:S(2)}, u32[]{:S(2)}) collective-permute-start(bf16[4,1,128,256]{3,2,1,0:T(8,128)(2,1)S(1)} %get-tuple-element.42), channel_id=1, source_target_pairs={{1,0},{2,1},{3,2},{5,4},{6,5},{7,6},{9,8},{10,9},{11,10},{13,12},{... | collective-permute-start | bytes 786440 | tf_op jit(solution)/shard_map/ppermute | solution.py:24
  54.4 1.4 %collective-permute-start.8 = (s32[16,8,128]{2,1,0:T(8,128)S(1)}, s32[16,8,128]{2,1,0:T(8,128)S(1)}, u32[]{:S(2)}, u32[]{:S(2)}) collective-permute-start(s32[16,8,128]{2,1,0:T(8,128)S(1)} %get-tuple-element.45.codes), channel_id=1, source_target_pairs={{0,16},{4,20},{8,24},{12,28},{16,0},{20,4},{24,8},{28,12},{1,17},{... | collective-permute-start | bytes 196616 | tf_op jit(solution)/shard_map/ppermute | solution.py:523
  55.7 2.8 %shard_map.83.partial = f32[2,4,128,256]{3,2,1,0:T(8,128)S(1)} custom-call(bf16[2,4,128,256]{3,2,1,0:T(8,128)(2,1)S(1)} %get-tuple-element.35.own, bf16[2,4,128,256]{3,2,1,0:T(8,128)(2,1)S(1)} %get-tuple-element.43.residual, bf16[3,3,3,256,256]{4,3,2,1,0:T(8,128)(2,1)S(1)} %copy-done, f32[8,128]{1,0:T(8,128)S(1)} %get-tuple-element.44._), custom_call_target="tpu_custom_call" | custom-call | tf_op jit(solution)/shard_map/pallas_call | solution.py:602
  58.5 0.9 collective-permute-done.8.others
  59.5 0.7 collective-permute-done.7.down
  60.1 4.7 %shard_map.84 = (bf16[2,4,128,256]{3,2,1,0:T(8,128)(2,1)S(1)}, bf16[2048,256]{1,0:T(8,128)(2,1)}, s32[32,8,128]{2,1,0:T(8,128)S(1)}, f32[8,128]{1,0:T(8,128)S(1)}) custom-call(bf16[2,4,128,256]{3,2,1,0:T(8,128)(2,1)S(1)} %collective-permute-done.4.before, bf16[4,1,128,256]{3,2,1,0:T(8,128)(2,1)S(1)} %collective-permute-done.6.up, ...), custom_call_target="tpu_custom_call" | custom-call | tf_op jit(solution)/shard_map/pallas_call | solution.py:610
  64.9 4.5 %all-to-all-start = ((bf16[32,64,256]{2,1,0:T(8,128)(2,1)}), bf16[32,64,256]{2,1,0:T(8,128)(2,1)S(1)}, u32[]{:S(2)}, u32[]{:S(2)}) async-start(bf16[32,64,256]{2,1,0:T(8,128)(2,1)} %bitcast.7), calls=%async_computation | async-start | bytes 2097152 | tf_op jit(solution)/shard_map/all_to_all | solution.py:619
  69.3 1.7 %collective-permute-start.9 = (bf16[512,256]{1,0:T(8,128)(2,1)S(1)}, bf16[512,256]{1,0:T(8,128)(2,1)S(1)}, u32[]{:S(2)}, u32[]{:S(2)}) collective-permute-start(bf16[512,256]{1,0:T(8,128)(2,1)S(1)} %get-tuple-element.49), channel_id=1, source_target_pairs={{0,1},{1,2},{2,3},{3,0},{4,5},{5,6},{6,7},{7,4},{8,9},{9,10},{10,1... | collective-permute-start | bytes 786440 | tf_op jit(solution)/shard_map/ppermute | solution.py:29
  71.6 4.9 %shard_map.85 = (bf16[512,256]{1,0:T(8,128)(2,1)S(1)}, f32[8,128]{1,0:T(8,128)}) custom-call(s32[32,64]{1,0:T(8,128)S(1)} %get-tuple-element.36.ask_ref, bf16[4096,16,256]{2,1,0:T(8,128)(2,1)} %bitcast.13, f32[64,32]{1,0:T(8,128)S(1)} %get-tuple-element.37.low_ref, f32[8,128]{1,0:T(8,128)S(1)} %get-tuple-element.47._), custom_call_target="tpu_custom_call" | custom-call | tf_op jit(solution)/shard_map/pallas_call | solution.py:585
  76.4 2.9 %shard_map.87 = (s32[32,128]{1,0:T(8,128)S(1)}, f32[1,2048]{1,0:T(1,128)S(1)}, s32[16,256]{1,0:T(8,128)S(1)}, f32[256,128]{1,0:T(8,128)S(1)}) custom-call(s32[1]{0:T(128)} %bitcast.6.near.here, s32[1]{0:T(128)} %bitcast.where_ref.here, s32[32,8,128]{2,1,0:T(8,128)S(1)} %get-tuple-element.52.every), custom_call_target="tpu_custom_call" | custom-call | tf_op jit(solution)/shard_map/pallas_call | solution.py:626
  79.4 4.5 %collective-permute-done.9.refs_1_ = bf16[512,256]{1,0:T(8,128)(2,1)S(1)} collective-permute-done((bf16[512,256]{1,0:T(8,128)(2,1)S(1)}, bf16[512,256]{1,0:T(8,128)(2,1)S(1)}, u32[]{:S(2)}, u32[]{:S(2)}) %collective-permute-start.9) | collective-permute-done | bytes 262176 | tf_op jit(solution)/shard_map/ppermute | solution.py:29
  83.9 9.8 %collective-permute-done.10.refs_2_ = bf16[512,256]{1,0:T(8,128)(2,1)S(1)} collective-permute-done((bf16[512,256]{1,0:T(8,128)(2,1)S(1)}, bf16[512,256]{1,0:T(8,128)(2,1)S(1)}, u32[]{:S(2)}, u32[]{:S(2)}) %collective-permute-start.10) | collective-permute-done | bytes 262176 | tf_op jit(solution)/shard_map/ppermute | solution.py:29
  93.6 0.6 collective-permute-done.11.refs_3_
  94.2 3.3 %shard_map.86 = bf16[1024,256]{1,0:T(8,128)(2,1)} custom-call(f32[8,1024]{1,0:T(8,128)S(1)} %get-tuple-element.30.refs_0_.place, bf16[1024,256]{1,0:T(8,128)(2,1)S(1)} %bitcast.11, bf16[1024,256]{1,0:T(8,128)(2,1)S(1)} %bitcast.10, bf16[512,256]{1,0:T(8,128)(2,1)S(1)} %get-tuple-element.48.refs_0_, bf16[512,256]{1,0:T(8,128)(2,1)S(1)} %collective-permute-done.9.refs_1_, ...), custom_call_target="tpu_custom_call" | custom-call | tf_op jit(solution)/shard_map/pallas_call | solution.py:639
  97.6 9.0 %shard_map.88 = bf16[8192,256]{1,0:T(8,128)(2,1)} custom-call(s32[1]{0:T(128)} %bitcast.6.near.here, s32[32,128]{1,0:T(8,128)S(1)} %get-tuple-element.53.bounds, bf16[2048,256]{1,0:T(8,128)(2,1)S(1)} %bitcast.9, bf16[65536,256]{1,0:T(8,128)(2,1)} %book.1, f32[1,2048]{1,0:T(1,128)S(1)} %get-tuple-element.55.order, s32[16,256]{1,0:T(8,128)S(1)} %get-tuple-element.56.codes, ...), custom_call_target="tpu_custom_call" | custom-call | tf_op jit(solution)/shard_map/pallas_call | solution.py:653
  (19 shorter events, 1.0 us)
Async XLA Ops:
  0.6 17.8 %collective-permute-start = (bf16[2,4,128,256]{3,2,1,0:T(8,128)(2,1)}, bf16[2,4,128,256]{3,2,1,0:T(8,128)(2,1)S(1)}, u32[]{:S(2)}, u32[]{:S(2)}) collective-permute-start(bf16[2,4,128,256]{3,2,1,0:T(8,128)(2,1)} %own.3), channel_id=1, source_target_pairs={{0,4},{4,8},{8,12},{12,16},{16,20},{20,24},{24,28},{1,5},{5,9},{9,... | collective-permute-start | bytes 1572872 | tf_op jit(solution)/shard_map/ppermute | solution.py:24
  11.7 2.0 %copy-start.1 = (bf16[3,3,3,256,256]{4,3,2,1,0:T(8,128)(2,1)S(1)}, bf16[3,3,3,256,256]{4,3,2,1,0:T(8,128)(2,1)}, u32[]{:S(2)}) copy-start(bf16[3,3,3,256,256]{4,3,2,1,0:T(8,128)(2,1)} %weight.5) | copy-start | bytes 10616836
  13.7 1.0 copy-start.3
  14.7 3.8 %copy-start.4 = (bf16[2,4,128,256]{3,2,1,0:T(8,128)(2,1)S(1)}, bf16[2,4,128,256]{3,2,1,0:T(8,128)(2,1)}, u32[]{:S(2)}) copy-start(bf16[2,4,128,256]{3,2,1,0:T(8,128)(2,1)} %own.3) | copy-start | bytes 1572868
  14.7 15.8 %copy-start.2 = (bf16[3,3,3,256,256]{4,3,2,1,0:T(8,128)(2,1)S(1)}, bf16[3,3,3,256,256]{4,3,2,1,0:T(8,128)(2,1)}, u32[]{:S(2)}) copy-start(bf16[3,3,3,256,256]{4,3,2,1,0:T(8,128)(2,1)} %weight.5) | copy-start | bytes 10616836
  19.5 7.8 %collective-permute-start.1 = (bf16[4,1,128,256]{3,2,1,0:T(8,128)(2,1)S(1)}, bf16[4,1,128,256]{3,2,1,0:T(8,128)(2,1)S(1)}, u32[]{:S(2)}, u32[]{:S(2)}) collective-permute-start(bf16[4,1,128,256]{3,2,1,0:T(8,128)(2,1)S(1)} %get-tuple-element.32), channel_id=1, source_target_pairs={{0,1},{1,2},{2,3},{4,5},{5,6},{6,7},{8,9},{9,10},{10,11},{12,13},{... | collective-permute-start | bytes 786440 | tf_op jit(solution)/shard_map/ppermute | solution.py:24
  22.8 7.7 %collective-permute-start.2 = (bf16[4,1,128,256]{3,2,1,0:T(8,128)(2,1)S(1)}, bf16[4,1,128,256]{3,2,1,0:T(8,128)(2,1)S(1)}, u32[]{:S(2)}, u32[]{:S(2)}) collective-permute-start(bf16[4,1,128,256]{3,2,1,0:T(8,128)(2,1)S(1)} %get-tuple-element.33), channel_id=1, source_target_pairs={{1,0},{2,1},{3,2},{5,4},{6,5},{7,6},{9,8},{10,9},{11,10},{13,12},{... | collective-permute-start | bytes 786440 | tf_op jit(solution)/shard_map/ppermute | solution.py:24
  24.7 2.7 %collective-permute-start.3 = (s32[4,8,128]{2,1,0:T(8,128)S(1)}, s32[4,8,128]{2,1,0:T(8,128)S(1)}, u32[]{:S(2)}, u32[]{:S(2)}) collective-permute-start(s32[4,8,128]{2,1,0:T(8,128)S(1)} %all_gather.3.codes_ref.codes.others), channel_id=1, source_target_pairs={{0,4},{4,0},{8,12},{12,8},{16,20},{20,16},{24,28},{28,24},{1,5},{5... | collective-permute-start | bytes 49160 | tf_op jit(solution)/shard_map/ppermute | solution.py:523
  34.5 12.5 %collective-permute-start.4 = (bf16[2,4,128,256]{3,2,1,0:T(8,128)(2,1)S(1)}, bf16[2,4,128,256]{3,2,1,0:T(8,128)(2,1)S(1)}, u32[]{:S(2)}, u32[]{:S(2)}) collective-permute-start(bf16[2,4,128,256]{3,2,1,0:T(8,128)(2,1)S(1)} %get-tuple-element.35.own), channel_id=1, source_target_pairs={{0,4},{4,8},{8,12},{12,16},{16,20},{20,24},{24,28},{1,5},{5,9},{9,... | collective-permute-start | bytes 1572872 | tf_op jit(solution)/shard_map/ppermute | solution.py:24
  37.6 9.3 %collective-permute-start.5 = (s32[8,8,128]{2,1,0:T(8,128)S(1)}, s32[8,8,128]{2,1,0:T(8,128)S(1)}, u32[]{:S(2)}, u32[]{:S(2)}) collective-permute-start(s32[8,8,128]{2,1,0:T(8,128)S(1)} %get-tuple-element.40.codes), channel_id=1, source_target_pairs={{0,8},{4,12},{8,0},{12,4},{16,24},{20,28},{24,16},{28,20},{1,9},{5... | collective-permute-start | bytes 98312 | tf_op jit(solution)/shard_map/ppermute | solution.py:523
  39.0 16.8 %copy-start = (bf16[3,3,3,256,256]{4,3,2,1,0:T(8,128)(2,1)S(1)}, bf16[3,3,3,256,256]{4,3,2,1,0:T(8,128)(2,1)}, u32[]{:S(2)}) copy-start(bf16[3,3,3,256,256]{4,3,2,1,0:T(8,128)(2,1)} %weight.7) | copy-start | bytes 10616836
  47.4 12.1 %collective-permute-start.6 = (bf16[4,1,128,256]{3,2,1,0:T(8,128)(2,1)S(1)}, bf16[4,1,128,256]{3,2,1,0:T(8,128)(2,1)S(1)}, u32[]{:S(2)}, u32[]{:S(2)}) collective-permute-start(bf16[4,1,128,256]{3,2,1,0:T(8,128)(2,1)S(1)} %get-tuple-element.41), channel_id=1, source_target_pairs={{0,1},{1,2},{2,3},{4,5},{5,6},{6,7},{8,9},{9,10},{10,11},{12,13},{... | collective-permute-start | bytes 786440 | tf_op jit(solution)/shard_map/ppermute | solution.py:24
  52.4 7.7 %collective-permute-start.7 = (bf16[4,1,128,256]{3,2,1,0:T(8,128)(2,1)S(1)}, bf16[4,1,128,256]{3,2,1,0:T(8,128)(2,1)S(1)}, u32[]{:S(2)}, u32[]{:S(2)}) collective-permute-start(bf16[4,1,128,256]{3,2,1,0:T(8,128)(2,1)S(1)} %get-tuple-element.42), channel_id=1, source_target_pairs={{1,0},{2,1},{3,2},{5,4},{6,5},{7,6},{9,8},{10,9},{11,10},{13,12},{... | collective-permute-start | bytes 786440 | tf_op jit(solution)/shard_map/ppermute | solution.py:24
  54.4 5.1 %collective-permute-start.8 = (s32[16,8,128]{2,1,0:T(8,128)S(1)}, s32[16,8,128]{2,1,0:T(8,128)S(1)}, u32[]{:S(2)}, u32[]{:S(2)}) collective-permute-start(s32[16,8,128]{2,1,0:T(8,128)S(1)} %get-tuple-element.45.codes), channel_id=1, source_target_pairs={{0,16},{4,20},{8,24},{12,28},{16,0},{20,4},{24,8},{28,12},{1,17},{... | collective-permute-start | bytes 196616 | tf_op jit(solution)/shard_map/ppermute | solution.py:523
  64.9 32.7 %all-to-all-start = ((bf16[32,64,256]{2,1,0:T(8,128)(2,1)}), bf16[32,64,256]{2,1,0:T(8,128)(2,1)S(1)}, u32[]{:S(2)}, u32[]{:S(2)}) async-start(bf16[32,64,256]{2,1,0:T(8,128)(2,1)} %bitcast.7), calls=%async_computation | async-start | bytes 2097152 | tf_op jit(solution)/shard_map/all_to_all | solution.py:619
  69.3 14.5 %collective-permute-start.9 = (bf16[512,256]{1,0:T(8,128)(2,1)S(1)}, bf16[512,256]{1,0:T(8,128)(2,1)S(1)}, u32[]{:S(2)}, u32[]{:S(2)}) collective-permute-start(bf16[512,256]{1,0:T(8,128)(2,1)S(1)} %get-tuple-element.49), channel_id=1, source_target_pairs={{0,1},{1,2},{2,3},{3,0},{4,5},{5,6},{6,7},{7,4},{8,9},{9,10},{10,1... | collective-permute-start | bytes 786440 | tf_op jit(solution)/shard_map/ppermute | solution.py:29
  71.0 22.6 %collective-permute-start.10 = (bf16[512,256]{1,0:T(8,128)(2,1)S(1)}, bf16[512,256]{1,0:T(8,128)(2,1)S(1)}, u32[]{:S(2)}, u32[]{:S(2)}) collective-permute-start(bf16[512,256]{1,0:T(8,128)(2,1)S(1)} %get-tuple-element.50), channel_id=1, source_target_pairs={{0,2},{1,3},{2,0},{3,1},{4,6},{5,7},{6,4},{7,5},{8,10},{9,11},{10,... | collective-permute-start | bytes 786440 | tf_op jit(solution)/shard_map/ppermute | solution.py:29
  71.0 23.2 %collective-permute-start.11 = (bf16[512,256]{1,0:T(8,128)(2,1)S(1)}, bf16[512,256]{1,0:T(8,128)(2,1)S(1)}, u32[]{:S(2)}, u32[]{:S(2)}) collective-permute-start(bf16[512,256]{1,0:T(8,128)(2,1)S(1)} %get-tuple-element.51), channel_id=1, source_target_pairs={{0,3},{1,0},{2,1},{3,2},{4,7},{5,4},{6,5},{7,6},{8,11},{9,8},{10,9... | collective-permute-start | bytes 786440 | tf_op jit(solution)/shard_map/ppermute | solution.py:29
  71.6 22.7 %copy-start.5 = (bf16[2,4,128,256]{3,2,1,0:T(8,128)(2,1)S(1)}, bf16[2,4,128,256]{3,2,1,0:T(8,128)(2,1)}, u32[]{:S(2)}) copy-start(bf16[2,4,128,256]{3,2,1,0:T(8,128)(2,1)} %param.11) | copy-start | bytes 1572868

commit v2 on v1

--- a/solution.py
+++ b/solution.py
@@ -52,6 +52,14 @@
 def finish(copies):
     for copy in copies:
         copy.wait()
+
+
+def rows16(width):
+    return lax.broadcasted_iota(jnp.int32, (BLOCK, width), 0).astype(jnp.int16)
+
+
+def onehot16(mask):
+    return jnp.where(mask, jnp.bfloat16(1), jnp.bfloat16(0))
 
 
 def onehot(mask):
@@ -209,15 +217,18 @@
     return taps(jnp.concatenate(pieces, axis=1), weight, columns).reshape(count, rows, columns, channels)
 
 
-def edge_taps(window, weight, side):
-    columns, channels = window.shape[2], window.shape[3]
-    row, q = (0, 0) if side == 0 else (window.shape[1] - 1, 2)
-    one, two = window[2, row], window[3, row]
-    before = jnp.concatenate([jnp.zeros_like(one), one], axis=0)
-    patch = jnp.concatenate([before, jnp.concatenate([one, two], axis=0)], axis=1)
+def edge_taps(edge, weight, q):
+    frames, columns, channels = edge.shape[0] - 2, edge.shape[2], edge.shape[3]
+    pieces = [edge[t : t + frames, 0].reshape(frames * columns, channels) for t in range(3)]
     return taps(
-        patch, lambda r: weight[1:, q, r].reshape(2 * channels, channels), columns
-    ).reshape(2, 1, columns, channels)
+        jnp.concatenate(pieces, axis=1), lambda r: weight[:, q, r].reshape(3 * channels, channels), columns
+    ).reshape(frames, 1, columns, channels)
+
+
+def earlier_taps(window, weight, result):
+    wide = 3 * window.shape[3]
+    result[...] += frame_taps(window, lambda r: weight[0, :, r].reshape(wide, -1), 0, 2)
+    result[0:1] += frame_taps(window, lambda r: weight[1, :, r].reshape(wide, -1), 1, 1)
 
 
 def own_kernel(change, own, residual, weight, *refs):
@@ -251,52 +262,59 @@
     finish(first + fetch([(result.at[1], partial.at[1])], sems.at[pl.ds(5, 1)]))
 
 
-def own_second_kernel(own, residual, weight, _, partial, window, source, result, sems):
+def earlier_kernel(before, own, weight, _, partial, window, result, sems):
+    frames, rows, columns, channels = result.shape
+    copies = fetch([(before, window.at[:, pl.ds(1, rows)]), (own, result)], sems)
+    empty = jnp.zeros((frames, 1, columns, channels), BF16)
+    window[:, 0:1] = empty
+    window[:, rows + 1 :] = empty
+    copies[0].wait()
+    for f in range(frames):
+        window[f, 1 : rows + 1] = act(window[f, 1 : rows + 1].astype(F32)).astype(BF16)
+    copies[1].wait()
+    earlier_taps(window, weight, result)
+    finish(fetch([(result, partial)], sems.at[pl.ds(2, 1)]))
+
+
+def both_kernel(before, own, residual, weight, _, partial, window, source, result, sems):
     frames, rows, columns, channels = source.shape
-    copies = fetch([(own, window.at[pl.ds(2, frames), pl.ds(1, rows)]), (residual, source)], sems)
-    empty = jnp.zeros((frames, 1, columns, channels), BF16)
-    window[2:, 0:1] = empty
-    window[2:, rows + 1 :] = empty
+    copies = fetch(
+        [
+            (own, window.at[pl.ds(2, frames), pl.ds(1, rows)]),
+            (residual, source),
+            (before, window.at[pl.ds(0, 2), pl.ds(1, rows)]),
+        ],
+        sems,
+    )
+    empty = jnp.zeros((frames + 2, 1, columns, channels), BF16)
+    window[:, 0:1] = empty
+    window[:, rows + 1 :] = empty
     finish(copies)
     wide = 3 * channels
     result[...] = source[...].astype(F32) + frame_taps(
         window, lambda r: weight[2, :, r].reshape(wide, channels), 2, 2
     )
-    first = fetch([(result.at[0], partial.at[0])], sems.at[pl.ds(2, 1)])
-    result[1] += frame_taps(window, lambda r: weight[1, :, r].reshape(wide, channels), 2, 1)[0]
-    finish(first + fetch([(result.at[1], partial.at[1])], sems.at[pl.ds(3, 1)]))
-
-
-def rest(change, before, up, down, partial, weight, window, total, sems):
-    frames, rows, columns, channels = total.shape
-    copies = fetch(
-        [
-            (before, window.at[pl.ds(0, 2), pl.ds(1, rows)]),
-            (up, window.at[:, pl.ds(0, 1)]),
-            (down, window.at[:, pl.ds(rows + 1, 1)]),
-            (partial, total),
-        ],
-        sems,
-    )
-    finish(copies[:3])
+    result[1:2] += frame_taps(window, lambda r: weight[1, :, r].reshape(wide, channels), 2, 1)
+    earlier_taps(window, weight, result)
+    finish(fetch([(result, partial)], sems.at[pl.ds(3, 1)]))
+
+
+def rest(change, up, down, partial, weight, edges, total, sems):
+    copies = fetch([(up, edges.at[0]), (down, edges.at[1]), (partial, total)], sems)
+    finish(copies[:2])
     if change:
-        for f in range(frames + 2):
-            for span in (slice(0, rows + 2),) if f < 2 else (slice(0, 1), slice(rows + 1, rows + 2)):
-                window[f, span] = act(window[f, span].astype(F32)).astype(BF16)
-    copies[3].wait()
-    wide = 3 * channels
-    total[...] += frame_taps(window, lambda r: weight[0, :, r].reshape(wide, channels), 0, 2)
-    total[0:1] += frame_taps(window, lambda r: weight[1, :, r].reshape(wide, channels), 1, 1)
-    total[:, 0:1] += edge_taps(window, weight, 0)
-    total[:, -1:] += edge_taps(window, weight, 1)
+        edges[...] = act(edges[...].astype(F32)).astype(BF16)
+    copies[2].wait()
+    total[:, 0:1] += edge_taps(edges.at[0], weight, 0)
+    total[:, -1:] += edge_taps(edges.at[1], weight, 2)
 
 
 def first_kernel(
-    before, up, down, partial, weight, codes, others, first, active, codes_out, done, window, total, a, b, sems
+    up, down, partial, weight, codes, others, first, active, codes_out, done, edges, total, a, b, sems
 ):
     done[...] = jnp.zeros_like(done)
     double(codes, others, codes_out)
-    rest(True, before, up, down, partial, weight, window, total, sems)
+    rest(True, up, down, partial, weight, edges, total, sems)
     outs = []
     for f in range(total.shape[0]):
         a[f] = total[f].astype(BF16)
@@ -307,21 +325,23 @@
     finish(outs)
 
 
-def second_kernel(before, up, down, partial, weight, place, codes, others, *refs):
-    encoded, terms, codes_out, done, window, total, a, packed, sems = refs
+def second_kernel(up, down, partial, weight, place, codes, others, *refs):
+    encoded, terms, codes_out, done, edges, total, a, packed, sems = refs
     done[...] = jnp.zeros_like(done)
     double(codes, others, codes_out)
-    rest(False, before, up, down, partial, weight, window, total, sems)
+    rest(False, up, down, partial, weight, edges, total, sems)
     frames, rows, columns, channels = total.shape
     a[...] = total[...].astype(BF16)
     outs = fetch([(a, encoded)], sems.at[pl.ds(4, 1)])
     flat = a[...].reshape(frames * rows * columns, channels)
     cells = flat.shape[0]
-    step = 256
+    step = BLOCK
+    at_slot = rows16(cells)
+    slot = place[0:1, :].astype(jnp.int32)
     for i in range(packed.shape[0] // step):
-        mine = lax.broadcasted_iota(jnp.int32, (step, cells), 0).astype(F32) + float(i * step) == place[0:1, :]
+        mine = onehot16(at_slot == (slot - i * step).astype(jnp.int16))
         span = pl.ds(i * step, step)
-        packed[span, :] = jnp.dot(onehot(mine), flat, preferred_element_type=F32).astype(BF16)
+        packed[span, :] = jnp.dot(mine, flat, preferred_element_type=F32).astype(BF16)
         outs.append(pltpu.make_async_copy(packed.at[span], terms.at[span], sems.at[5 + i]))
         outs[-1].start()
     finish(outs)
@@ -436,42 +456,32 @@
     blocks = out.shape[0] // BLOCK
     own = pl.ds(pl.multiple_of(here[0] * out.shape[0], BLOCK), out.shape[0])
     copies = fetch([(terms, rows_in), (book.at[own], book_in)], sems)
+    ranked[slots:, :] = jnp.zeros((ranked.shape[0] - slots, ranked.shape[1]), BF16)
+    at_slot = rows16(slots)
+    place = order[...].astype(jnp.int32)
     copies[0].wait()
-    at_slot = lax.broadcasted_iota(jnp.int32, (BLOCK, slots), 0).astype(F32)
-
-    def rank(i, carry):
-        mine = onehot(at_slot == order[...] - (i * BLOCK).astype(F32))
-        span = pl.ds(pl.multiple_of(i * BLOCK, BLOCK), BLOCK)
+    for i in range(chunks):
+        span = slice(i * BLOCK, (i + 1) * BLOCK)
+        mine = onehot16(at_slot == (place - i * BLOCK).astype(jnp.int16))
         ranked[span, :] = jnp.dot(mine, rows_in[...], preferred_element_type=F32).astype(BF16)
-        return carry
-
-    lax.fori_loop(0, chunks, rank, 0)
-    ranked[slots:, :] = jnp.zeros((ranked.shape[0] - slots, ranked.shape[1]), BF16)
     copies[1].wait()
-    at_row = lax.broadcasted_iota(jnp.int32, (BLOCK, BLOCK), 0)
-    step = 8
-
-    def part(b, j):
-        mine = onehot(at_row == codes[pl.ds(j, 1), :] - b * BLOCK)
-        rows = ranked[pl.ds(pl.multiple_of(j * BLOCK, BLOCK), BLOCK), :]
+    at_row = rows16(2 * BLOCK)
+
+    def two(b, j):
+        code = jnp.concatenate([codes[pl.ds(j, 1), :], codes[pl.ds(j + 1, 1), :]], axis=1)
+        mine = onehot16(at_row == (code - b * BLOCK).astype(jnp.int16))
+        rows = ranked[pl.ds(pl.multiple_of(j * BLOCK, BLOCK), 2 * BLOCK), :]
         return jnp.dot(mine, rows, preferred_element_type=F32)
 
     def leave(b):
         span = pl.ds(pl.multiple_of(b * BLOCK, BLOCK), BLOCK)
         return pltpu.make_async_copy(out.at[span], grad.at[span], sems.at[2 + b])
 
-    def several(g, carry):
-        counts = pltpu.roll(named[...], lax.rem(named.shape[1] - g * step, named.shape[1]), 1)
-        for i in range(step):
-            b = g * step + i
-            first = bounds[b, 0] // BLOCK
-            span = pl.ds(pl.multiple_of(b * BLOCK, BLOCK), BLOCK)
-            total = part(b, first) + part(b, first + 1)
-            out[span, :] = (2.0 * (counts[:, i : i + 1] * book_in[span, :].astype(F32) - total)).astype(BF16)
-            leave(b).start()
-        return carry
-
-    lax.fori_loop(0, blocks // step, several, 0)
+    for b in range(blocks):
+        span = slice(b * BLOCK, (b + 1) * BLOCK)
+        total = two(b, bounds[b, 0] // BLOCK)
+        out[span, :] = (2.0 * (named[:, b : b + 1] * book_in[span, :].astype(F32) - total)).astype(BF16)
+        leave(b).start()
 
     def last(b, carry):
         first = bounds[b, 0] // BLOCK
@@ -483,11 +493,11 @@
             span = pl.ds(pl.multiple_of(b * BLOCK, BLOCK), BLOCK)
             sums[...] = jnp.zeros_like(sums)
 
-            def more(j, carry):
-                sums[...] += part(b, j)
+            def more(i, carry):
+                sums[...] += two(b, first + 2 * i)
                 return carry
 
-            lax.fori_loop(first, after, more, 0)
+            lax.fori_loop(0, (after - first + 1) // 2, more, 0)
             counts = pltpu.roll(named[...], lax.rem(named.shape[1] - b, named.shape[1]), 1)
             out[span, :] = (2.0 * (counts[:, 0:1] * book_in[span, :].astype(F32) - sums[...])).astype(BF16)
             leave(b).start()
@@ -535,6 +545,7 @@
     slots = owners * capacity
     block = (frames, rows, columns, channels)
     window = pltpu.VMEM((frames + 2, rows + 2, columns, channels), BF16)
+    edges = pltpu.VMEM((2, frames + 2, 1, columns, channels), BF16)
     whole = pltpu.VMEM(block, F32)
     half = pltpu.VMEM(block, BF16)
     token = shape((8, 128), F32)
@@ -571,14 +582,22 @@
         compiler_params=params(28),
     )(latents, latents, conv_first, place)
     before, up, down, _, done = halo(latents, done, shared, shared)
+    partial = pl.pallas_call(
+        earlier_kernel,
+        out_shape=shape(block, F32),
+        in_specs=[HBM] * 2 + [VMEM] * 2,
+        out_specs=HBM,
+        scratch_shapes=[pltpu.VMEM((2, rows + 2, columns, channels), BF16), whole, sems((3,))],
+        compiler_params=params(),
+    )(before, partial, conv_first, done)
     first, active, every, done = pl.pallas_call(
         first_kernel,
         out_shape=(shape(block), shape(block), code_lines(2 * by), token),
-        in_specs=[HBM] * 4 + [VMEM] * 3,
+        in_specs=[HBM] * 3 + [VMEM] * 3,
         out_specs=(HBM, HBM, VMEM, VMEM),
-        scratch_shapes=[window, whole, half, half, sems((4 + 2 * frames,))],
-        compiler_params=params(),
-    )(before, up, down, partial, conv_first, every, swapped(every, "tm", by))
+        scratch_shapes=[edges, whole, half, half, sems((4 + 2 * frames,))],
+        compiler_params=params(),
+    )(up, down, partial, conv_first, every, swapped(every, "tm", by))
     by *= 2
 
     def lookup(which, after):
@@ -600,21 +619,21 @@
     before, up, down, every, done = halo(active, done, every, swapped(every, "tm", by))
     by *= 2
     partial = pl.pallas_call(
-        own_second_kernel,
+        both_kernel,
         out_shape=shape(block, F32),
-        in_specs=[HBM] * 2 + [VMEM] * 2,
+        in_specs=[HBM] * 3 + [VMEM] * 2,
         out_specs=HBM,
         scratch_shapes=[window, half, whole, sems((4,))],
         compiler_params=params(),
-    )(active, first, conv_second, done)
+    )(before, active, first, conv_second, done)
     encoded, terms, every, done = pl.pallas_call(
         second_kernel,
         out_shape=(shape(block), shape((slots, channels)), code_lines(2 * by), token),
-        in_specs=[HBM] * 4 + [VMEM] * 4,
+        in_specs=[HBM] * 3 + [VMEM] * 4,
         out_specs=(HBM, HBM, VMEM, VMEM),
-        scratch_shapes=[window, whole, half, pltpu.VMEM((slots, channels), BF16), sems((5 + slots // 256,))],
-        compiler_params=params(),
-    )(before, up, down, partial, conv_second, place, every, swapped(every, "tm", by))
+        scratch_shapes=[edges, whole, half, pltpu.VMEM((slots, channels), BF16), sems((5 + slots // 256,))],
+        compiler_params=params(),
+    )(up, down, partial, conv_second, place, every, swapped(every, "tm", by))
 
     owner_terms = lax.all_to_all(
         terms.reshape(owners, capacity, channels), ("tm", "height"), split_axis=0, concat_axis=0, tiled=True

time: 107 us -> 102 us (0.953)
  waiting for transfers between devices: 20.9 us -> 17.4 us
  Pallas kernels: 45.8 us -> 43.9 us
    pallas_call x1 -> x2, Pallas kernels: 2.81 us -> 6.89 us  [the longest x1 4.17 us: on_device(): pl.pallas_call(both_kernel, out_shape=shape(block, F32), in_specs=[HBM] *...]
    ppermute x3, starting transfers between devices: 3.97 us -> 6.81 us  [swapped(): return lax.ppermute(codes, axis, [(i, i ^ by) for i in range(count)])]
    ppermute x6, starting transfers between devices: 19.3 us -> 16.6 us  [along(): lax.ppermute(x, axis, [(i, i + by) for i in range(count) if 0 <= i + by <...]
    ppermute x3, waiting for transfers between devices: 2.3 us -> 0.01 us  [swapped(): return lax.ppermute(codes, axis, [(i, i ^ by) for i in range(count)])]
    pallas_call x1, Pallas kernels: 9.01 us -> 6.72 us  [on_device(): pl.pallas_call(scatter_kernel, out_shape=shape((range_rows, channels)), i...]
    pallas_call x1, Pallas kernels: 4 us -> 1.91 us  [on_device(): pl.pallas_call(first_kernel, out_shape=(shape(block), shape(block), code_...]
    ppermute x6, waiting for transfers between devices: 3.78 us -> 1.75 us  [along(): lax.ppermute(x, axis, [(i, i + by) for i in range(count) if 0 <= i + by <...]
    pallas_call x1, Pallas kernels: 4.73 us -> 3.06 us  [on_device(): pl.pallas_call(second_kernel, out_shape=(shape(block), shape((slots, chan...]
  transfers between devices with their start and end apart: 13 -> 13, of which waited for: 7 -> 4; matrix products, arithmetic and copies ran while one was open for 0% -> 0% of each run, Pallas kernels for 25% -> 30%
where the time goes in v2:
time: 102 us; the launch traced here: 101 us
  Pallas kernels  43.9 us (43%)
  starting transfers between devices  29.7 us (29%)
  waiting for transfers between devices  17.4 us (17%)
  blocking collectives  6.07 us (6%)
  local copies, waits for them, and re-layouts  3.05 us (3%)
  between operations  1.05 us (1%)
    ppermute x6, starting transfers between devices, along(): lax.ppermute(x, axis, [(i, i + by) for i in range(count) if 0 <= i + by <...  16.6 us
    ppermute x3, waiting for transfers between devices, around(): return lax.ppermute(x, axis, [(i, (i + by) % count) for i in range(count)])  15.7 us
    pallas_call x2, Pallas kernels, lookup(): pl.pallas_call(functools.partial(gather_kernel, which), out_shape=(shape(...  12.9 us
    ppermute x3, starting transfers between devices, swapped(): return lax.ppermute(codes, axis, [(i, i ^ by) for i in range(count)])  6.81 us
    pallas_call x1, Pallas kernels, on_device(): pl.pallas_call(scatter_kernel, out_shape=shape((range_rows, channels)), i...  6.72 us
    all_gather x1, blocking collectives, on_device(): shared = lax.all_gather(codes.reshape(frames * rows, columns), 'height')  6.07 us
    pallas_call x1, Pallas kernels, on_device(): pl.pallas_call(both_kernel, out_shape=shape(block, F32), in_specs=[HBM] *...  4.17 us
    all_to_all x1, starting transfers between devices, on_device(): lax.all_to_all(terms.reshape(owners, capacity, channels), ('tm', 'height'...  4.01 us
  transfers between devices with their start and end apart: 13, of which 4 were waited for; matrix products, arithmetic and copies ran while one was open for 0% of the time, Pallas kernels for 30%

profile of v2, /device:TPU:1, one launch (start us, length us, event | category | flops | bytes accessed | tf_op | source)
XLA Modules:
  0.0 101.2 jit_solution(5826732774459938786)
XLA Ops:
  0.6 4.0 %collective-permute-start = (bf16[2,4,128,256]{3,2,1,0:T(8,128)(2,1)}, bf16[2,4,128,256]{3,2,1,0:T(8,128)(2,1)S(1)}, u32[]{:S(2)}, u32[]{:S(2)}) collective-permute-start(bf16[2,4,128,256]{3,2,1,0:T(8,128)(2,1)} %own.3), channel_id=1, source_target_pairs={{0,4},{4,8},{8,12},{12,16},{16,20},{20,24},{24,28},{1,5},{5,9},{9,... | collective-permute-start | bytes 1572872 | tf_op jit(solution)/shard_map/ppermute | solution.py:24
  4.6 6.1 %all_gather.3.codes_ref.codes.others = s32[4,8,128]{2,1,0:T(8,128)S(1)} all-gather(s32[1,8,128]{2,1,0:T(8,128)} %bitcast.15), channel_id=1, replica_groups=mesh['tm'=8,'height'=4] {'height'}, dimensions={0}, use_global_device_ids=true | all-gather | bytes 20480 | tf_op jit(solution)/shard_map/all_gather | solution.py:559
  10.7 0.9 shard_map.77
  11.7 2.0 %copy-done = bf16[3,3,3,256,256]{4,3,2,1,0:T(8,128)(2,1)S(1)} copy-done((bf16[3,3,3,256,256]{4,3,2,1,0:T(8,128)(2,1)S(1)}, bf16[3,3,3,256,256]{4,3,2,1,0:T(8,128)(2,1)}, u32[]{:S(2)}) %copy-start) | copy-done | bytes 3538968
  13.7 1.0 %copy-done.3 = bf16[2,4,128,256]{3,2,1,0:T(8,128)(2,1)S(1)} copy-done((bf16[2,4,128,256]{3,2,1,0:T(8,128)(2,1)S(1)}, bf16[2,4,128,256]{3,2,1,0:T(8,128)(2,1)}, u32[]{:S(2)}) %copy-start.3) | copy-done | bytes 524312
  14.7 3.7 %shard_map.78 = (f32[2,4,128,256]{3,2,1,0:T(8,128)S(1)}, f32[8,128]{1,0:T(8,128)S(1)}) custom-call(bf16[2,4,128,256]{3,2,1,0:T(8,128)(2,1)S(1)} %copy-done.3, bf16[2,4,128,256]{3,2,1,0:T(8,128)(2,1)S(1)} %copy-done.3, bf16[3,3,3,256,256]{4,3,2,1,0:T(8,128)(2,1)S(1)} %copy-done, f32[8,1024]{1,0:T(8,128)S(1)} %get-tuple-element.31.refs_0_.place), custom_call_target="tpu_custom_call" | custom-call | tf_op jit(solution)/shard_map/pallas_call | solution.py:576
  18.5 1.1 %shard_map.79 = (bf16[4,1,128,256]{3,2,1,0:T(8,128)(2,1)S(1)}, bf16[4,1,128,256]{3,2,1,0:T(8,128)(2,1)S(1)}, s32[8,8,128]{2,1,0:T(8,128)}, f32[8,128]{1,0:T(8,128)S(1)}) custom-call(bf16[2,4,128,256]{3,2,1,0:T(8,128)(2,1)S(1)} %collective-permute-done.before, bf16[2,4,128,256]{3,2,1,0:T(8,128)(2,1)S(1)} %copy-done.4, f32[8,128]{1,0:T(8,128)S(1)} %get-tuple-element.32._, ...), custom_call_target="tpu_custom_call" | custom-call | tf_op jit(solution)/shard_map/pallas_call | solution.py:520
  19.5 3.2 %collective-permute-start.1 = (bf16[4,1,128,256]{3,2,1,0:T(8,128)(2,1)S(1)}, bf16[4,1,128,256]{3,2,1,0:T(8,128)(2,1)S(1)}, u32[]{:S(2)}, u32[]{:S(2)}) collective-permute-start(bf16[4,1,128,256]{3,2,1,0:T(8,128)(2,1)S(1)} %get-tuple-element.33), channel_id=1, source_target_pairs={{0,1},{1,2},{2,3},{4,5},{5,6},{6,7},{8,9},{9,10},{10,11},{12,13},{... | collective-permute-start | bytes 786440 | tf_op jit(solution)/shard_map/ppermute | solution.py:24
  22.8 1.9 %collective-permute-start.2 = (bf16[4,1,128,256]{3,2,1,0:T(8,128)(2,1)S(1)}, bf16[4,1,128,256]{3,2,1,0:T(8,128)(2,1)S(1)}, u32[]{:S(2)}, u32[]{:S(2)}) collective-permute-start(bf16[4,1,128,256]{3,2,1,0:T(8,128)(2,1)S(1)} %get-tuple-element.34), channel_id=1, source_target_pairs={{1,0},{2,1},{3,2},{5,4},{6,5},{7,6},{9,8},{10,9},{11,10},{13,12},{... | collective-permute-start | bytes 786440 | tf_op jit(solution)/shard_map/ppermute | solution.py:24
  24.7 1.3 %collective-permute-start.3 = (s32[4,8,128]{2,1,0:T(8,128)S(1)}, s32[4,8,128]{2,1,0:T(8,128)S(1)}, u32[]{:S(2)}, u32[]{:S(2)}) collective-permute-start(s32[4,8,128]{2,1,0:T(8,128)S(1)} %all_gather.3.codes_ref.codes.others), channel_id=1, source_target_pairs={{0,4},{4,0},{8,12},{12,8},{16,20},{20,16},{24,28},{28,24},{1,5},{5... | collective-permute-start | bytes 49160 | tf_op jit(solution)/shard_map/ppermute | solution.py:533
  26.0 2.7 %shard_map.80.partial = f32[2,4,128,256]{3,2,1,0:T(8,128)S(1)} custom-call(bf16[2,4,128,256]{3,2,1,0:T(8,128)(2,1)S(1)} %collective-permute-done.before, f32[2,4,128,256]{3,2,1,0:T(8,128)S(1)} %get-tuple-element.35.own, bf16[3,3,3,256,256]{4,3,2,1,0:T(8,128)(2,1)S(1)} %copy-done.1, f32[8,128]{1,0:T(8,128)S(1)} %get-tuple-element.36._), custom_call_target="tpu_custom_call" | custom-call | tf_op jit(solution)/shard_map/pallas_call | solution.py:585
  28.7 1.7 %collective-permute-done.2.down = bf16[4,1,128,256]{3,2,1,0:T(8,128)(2,1)S(1)} collective-permute-done((bf16[4,1,128,256]{3,2,1,0:T(8,128)(2,1)S(1)}, bf16[4,1,128,256]{3,2,1,0:T(8,128)(2,1)S(1)}, u32[]{:S(2)}, u32[]{:S(2)}) %collective-permute-start.2) | collective-permute-done | bytes 262176 | tf_op jit(solution)/shard_map/ppermute | solution.py:24
  30.5 1.9 %shard_map.81 = (bf16[2,4,128,256]{3,2,1,0:T(8,128)(2,1)S(1)}, bf16[2,4,128,256]{3,2,1,0:T(8,128)(2,1)S(1)}, s32[8,8,128]{2,1,0:T(8,128)S(1)}, f32[8,128]{1,0:T(8,128)S(1)}) custom-call(bf16[4,1,128,256]{3,2,1,0:T(8,128)(2,1)S(1)} %collective-permute-done.1.up, bf16[4,1,128,256]{3,2,1,0:T(8,128)(2,1)S(1)} %collective-permute-done.2.down, ...), custom_call_target="tpu_custom_call" | custom-call | tf_op jit(solution)/shard_map/pallas_call | solution.py:593
  32.4 3.1 %collective-permute-start.4 = (bf16[2,4,128,256]{3,2,1,0:T(8,128)(2,1)S(1)}, bf16[2,4,128,256]{3,2,1,0:T(8,128)(2,1)S(1)}, u32[]{:S(2)}, u32[]{:S(2)}) collective-permute-start(bf16[2,4,128,256]{3,2,1,0:T(8,128)(2,1)S(1)} %get-tuple-element.37.own), channel_id=1, source_target_pairs={{0,4},{4,8},{8,12},{12,16},{16,20},{20,24},{24,28},{1,5},{5,9},{9,... | collective-permute-start | bytes 1572872 | tf_op jit(solution)/shard_map/ppermute | solution.py:24
  35.5 1.3 %collective-permute-start.5 = (s32[8,8,128]{2,1,0:T(8,128)S(1)}, s32[8,8,128]{2,1,0:T(8,128)S(1)}, u32[]{:S(2)}, u32[]{:S(2)}) collective-permute-start(s32[8,8,128]{2,1,0:T(8,128)S(1)} %get-tuple-element.42.codes), channel_id=1, source_target_pairs={{0,8},{4,12},{8,0},{12,4},{16,24},{20,28},{24,16},{28,20},{1,9},{5... | collective-permute-start | bytes 98312 | tf_op jit(solution)/shard_map/ppermute | solution.py:533
  36.9 8.8 %shard_map.82 = (bf16[512,256]{1,0:T(8,128)(2,1)S(1)}, bf16[512,256]{1,0:T(8,128)(2,1)S(1)}, bf16[512,256]{1,0:T(8,128)(2,1)S(1)}, f32[8,128]{1,0:T(8,128)S(1)}) custom-call(s32[32,64]{1,0:T(8,128)S(1)} %get-tuple-element.38.ask_ref, bf16[4096,16,256]{2,1,0:T(8,128)(2,1)} %bitcast.12, f32[64,32]{1,0:T(8,128)S(1)} %get-tuple-element.39.low_ref, ...), custom_call_target="tpu_custom_call" | custom-call | tf_op jit(solution)/shard_map/pallas_call | solution.py:604
  45.7 0.4 shard_map.83
  46.2 2.3 %collective-permute-start.6 = (bf16[4,1,128,256]{3,2,1,0:T(8,128)(2,1)S(1)}, bf16[4,1,128,256]{3,2,1,0:T(8,128)(2,1)S(1)}, u32[]{:S(2)}, u32[]{:S(2)}) collective-permute-start(bf16[4,1,128,256]{3,2,1,0:T(8,128)(2,1)S(1)} %get-tuple-element.43), channel_id=1, source_target_pairs={{0,1},{1,2},{2,3},{4,5},{5,6},{6,7},{8,9},{9,10},{10,11},{12,13},{... | collective-permute-start | bytes 786440 | tf_op jit(solution)/shard_map/ppermute | solution.py:24
  48.5 2.0 %collective-permute-start.7 = (bf16[4,1,128,256]{3,2,1,0:T(8,128)(2,1)S(1)}, bf16[4,1,128,256]{3,2,1,0:T(8,128)(2,1)S(1)}, u32[]{:S(2)}, u32[]{:S(2)}) collective-permute-start(bf16[4,1,128,256]{3,2,1,0:T(8,128)(2,1)S(1)} %get-tuple-element.44), channel_id=1, source_target_pairs={{1,0},{2,1},{3,2},{5,4},{6,5},{7,6},{9,8},{10,9},{11,10},{13,12},{... | collective-permute-start | bytes 786440 | tf_op jit(solution)/shard_map/ppermute | solution.py:24
  50.5 4.2 %collective-permute-start.8 = (s32[16,8,128]{2,1,0:T(8,128)S(1)}, s32[16,8,128]{2,1,0:T(8,128)S(1)}, u32[]{:S(2)}, u32[]{:S(2)}) collective-permute-start(s32[16,8,128]{2,1,0:T(8,128)S(1)} %get-tuple-element.47.codes), channel_id=1, source_target_pairs={{0,16},{4,20},{8,24},{12,28},{16,0},{20,4},{24,8},{28,12},{1,17},{... | collective-permute-start | bytes 196616 | tf_op jit(solution)/shard_map/ppermute | solution.py:533
  54.7 4.2 %shard_map.84.partial = f32[2,4,128,256]{3,2,1,0:T(8,128)S(1)} custom-call(bf16[2,4,128,256]{3,2,1,0:T(8,128)(2,1)S(1)} %collective-permute-done.4.before, bf16[2,4,128,256]{3,2,1,0:T(8,128)(2,1)S(1)} %get-tuple-element.37.own, bf16[2,4,128,256]{3,2,1,0:T(8,128)(2,1)S(1)} %get-tuple-element.45.residual, bf16[3,3,3,256,256]{4,3,2,1,0:T(8,128)(2,1)S(1)} %copy-done.2, ...), custom_call_target="tpu_custom_call" | custom-call | tf_op jit(solution)/shard_map/pallas_call | solution.py:621
  59.0 3.1 %shard_map.85 = (bf16[2,4,128,256]{3,2,1,0:T(8,128)(2,1)S(1)}, bf16[2048,256]{1,0:T(8,128)(2,1)}, s32[32,8,128]{2,1,0:T(8,128)S(1)}, f32[8,128]{1,0:T(8,128)S(1)}) custom-call(bf16[4,1,128,256]{3,2,1,0:T(8,128)(2,1)S(1)} %collective-permute-done.6.up, bf16[4,1,128,256]{3,2,1,0:T(8,128)(2,1)S(1)} %collective-permute-done.7.down, ...), custom_call_target="tpu_custom_call" | custom-call | tf_op jit(solution)/shard_map/pallas_call | solution.py:629
  62.0 4.0 %all-to-all-start = ((bf16[32,64,256]{2,1,0:T(8,128)(2,1)}), bf16[32,64,256]{2,1,0:T(8,128)(2,1)S(1)}, u32[]{:S(2)}, u32[]{:S(2)}) async-start(bf16[32,64,256]{2,1,0:T(8,128)(2,1)} %bitcast.7), calls=%async_computation | async-start | bytes 2097152 | tf_op jit(solution)/shard_map/all_to_all | solution.py:638
  66.0 1.7 %collective-permute-start.9 = (bf16[512,256]{1,0:T(8,128)(2,1)S(1)}, bf16[512,256]{1,0:T(8,128)(2,1)S(1)}, u32[]{:S(2)}, u32[]{:S(2)}) collective-permute-start(bf16[512,256]{1,0:T(8,128)(2,1)S(1)} %get-tuple-element.51), channel_id=1, source_target_pairs={{0,1},{1,2},{2,3},{3,0},{4,5},{5,6},{6,7},{7,4},{8,9},{9,10},{10,1... | collective-permute-start | bytes 786440 | tf_op jit(solution)/shard_map/ppermute | solution.py:29
  67.7 0.5 collective-permute-start.11
  68.3 4.0 %shard_map.86 = (bf16[512,256]{1,0:T(8,128)(2,1)S(1)}, f32[8,128]{1,0:T(8,128)}) custom-call(s32[32,64]{1,0:T(8,128)S(1)} %get-tuple-element.38.ask_ref, bf16[4096,16,256]{2,1,0:T(8,128)(2,1)} %bitcast.13, f32[64,32]{1,0:T(8,128)S(1)} %get-tuple-element.39.low_ref, f32[8,128]{1,0:T(8,128)S(1)} %get-tuple-element.49._), custom_call_target="tpu_custom_call" | custom-call | tf_op jit(solution)/shard_map/pallas_call | solution.py:604
  72.3 2.9 %shard_map.88 = (s32[32,128]{1,0:T(8,128)S(1)}, f32[1,2048]{1,0:T(1,128)S(1)}, s32[16,256]{1,0:T(8,128)S(1)}, f32[256,128]{1,0:T(8,128)S(1)}) custom-call(s32[1]{0:T(128)} %bitcast.6.near.here, s32[1]{0:T(128)} %bitcast.where_ref.here, s32[32,8,128]{2,1,0:T(8,128)S(1)} %get-tuple-element.54.every), custom_call_target="tpu_custom_call" | custom-call | tf_op jit(solution)/shard_map/pallas_call | solution.py:645
  75.3 5.3 %collective-permute-done.9.refs_1_ = bf16[512,256]{1,0:T(8,128)(2,1)S(1)} collective-permute-done((bf16[512,256]{1,0:T(8,128)(2,1)S(1)}, bf16[512,256]{1,0:T(8,128)(2,1)S(1)}, u32[]{:S(2)}, u32[]{:S(2)}) %collective-permute-start.9) | collective-permute-done | bytes 262176 | tf_op jit(solution)/shard_map/ppermute | solution.py:29
  80.6 9.8 %collective-permute-done.10.refs_2_ = bf16[512,256]{1,0:T(8,128)(2,1)S(1)} collective-permute-done((bf16[512,256]{1,0:T(8,128)(2,1)S(1)}, bf16[512,256]{1,0:T(8,128)(2,1)S(1)}, u32[]{:S(2)}, u32[]{:S(2)}) %collective-permute-start.10) | collective-permute-done | bytes 262176 | tf_op jit(solution)/shard_map/ppermute | solution.py:29
  90.3 0.6 collective-permute-done.11.refs_3_
  90.9 3.4 %shard_map.87 = bf16[1024,256]{1,0:T(8,128)(2,1)} custom-call(f32[8,1024]{1,0:T(8,128)S(1)} %get-tuple-element.31.refs_0_.place, bf16[1024,256]{1,0:T(8,128)(2,1)S(1)} %bitcast.11, bf16[1024,256]{1,0:T(8,128)(2,1)S(1)} %bitcast.10, bf16[512,256]{1,0:T(8,128)(2,1)S(1)} %get-tuple-element.50.refs_0_, bf16[512,256]{1,0:T(8,128)(2,1)S(1)} %collective-permute-done.9.refs_1_, ...), custom_call_target="tpu_custom_call" | custom-call | tf_op jit(solution)/shard_map/pallas_call | solution.py:658
  94.3 6.7 %shard_map.89 = bf16[8192,256]{1,0:T(8,128)(2,1)} custom-call(s32[1]{0:T(128)} %bitcast.6.near.here, s32[32,128]{1,0:T(8,128)S(1)} %get-tuple-element.55.bounds, bf16[2048,256]{1,0:T(8,128)(2,1)S(1)} %bitcast.9, bf16[65536,256]{1,0:T(8,128)(2,1)} %book.1, f32[1,2048]{1,0:T(1,128)S(1)} %get-tuple-element.57.order, s32[16,256]{1,0:T(8,128)S(1)} %get-tuple-element.58.codes, ...), custom_call_target="tpu_custom_call" | custom-call | tf_op jit(solution)/shard_map/pallas_call | solution.py:672
  (20 shorter events, 0.0 us)
Async XLA Ops:
  0.6 17.8 %collective-permute-start = (bf16[2,4,128,256]{3,2,1,0:T(8,128)(2,1)}, bf16[2,4,128,256]{3,2,1,0:T(8,128)(2,1)S(1)}, u32[]{:S(2)}, u32[]{:S(2)}) collective-permute-start(bf16[2,4,128,256]{3,2,1,0:T(8,128)(2,1)} %own.3), channel_id=1, source_target_pairs={{0,4},{4,8},{8,12},{12,16},{16,20},{20,24},{24,28},{1,5},{5,9},{9,... | collective-permute-start | bytes 1572872 | tf_op jit(solution)/shard_map/ppermute | solution.py:24
  11.7 2.0 %copy-start = (bf16[3,3,3,256,256]{4,3,2,1,0:T(8,128)(2,1)S(1)}, bf16[3,3,3,256,256]{4,3,2,1,0:T(8,128)(2,1)}, u32[]{:S(2)}) copy-start(bf16[3,3,3,256,256]{4,3,2,1,0:T(8,128)(2,1)} %weight.7) | copy-start | bytes 10616836
  13.7 1.0 %copy-start.3 = (bf16[2,4,128,256]{3,2,1,0:T(8,128)(2,1)S(1)}, bf16[2,4,128,256]{3,2,1,0:T(8,128)(2,1)}, u32[]{:S(2)}) copy-start(bf16[2,4,128,256]{3,2,1,0:T(8,128)(2,1)} %own.3) | copy-start | bytes 1572868
  14.7 3.8 %copy-start.4 = (bf16[2,4,128,256]{3,2,1,0:T(8,128)(2,1)S(1)}, bf16[2,4,128,256]{3,2,1,0:T(8,128)(2,1)}, u32[]{:S(2)}) copy-start(bf16[2,4,128,256]{3,2,1,0:T(8,128)(2,1)} %own.3) | copy-start | bytes 1572868
  14.7 11.3 %copy-start.1 = (bf16[3,3,3,256,256]{4,3,2,1,0:T(8,128)(2,1)S(1)}, bf16[3,3,3,256,256]{4,3,2,1,0:T(8,128)(2,1)}, u32[]{:S(2)}) copy-start(bf16[3,3,3,256,256]{4,3,2,1,0:T(8,128)(2,1)} %weight.7) | copy-start | bytes 10616836
  19.5 9.2 %collective-permute-start.1 = (bf16[4,1,128,256]{3,2,1,0:T(8,128)(2,1)S(1)}, bf16[4,1,128,256]{3,2,1,0:T(8,128)(2,1)S(1)}, u32[]{:S(2)}, u32[]{:S(2)}) collective-permute-start(bf16[4,1,128,256]{3,2,1,0:T(8,128)(2,1)S(1)} %get-tuple-element.33), channel_id=1, source_target_pairs={{0,1},{1,2},{2,3},{4,5},{5,6},{6,7},{8,9},{9,10},{10,11},{12,13},{... | collective-permute-start | bytes 786440 | tf_op jit(solution)/shard_map/ppermute | solution.py:24
  22.8 7.7 %collective-permute-start.2 = (bf16[4,1,128,256]{3,2,1,0:T(8,128)(2,1)S(1)}, bf16[4,1,128,256]{3,2,1,0:T(8,128)(2,1)S(1)}, u32[]{:S(2)}, u32[]{:S(2)}) collective-permute-start(bf16[4,1,128,256]{3,2,1,0:T(8,128)(2,1)S(1)} %get-tuple-element.34), channel_id=1, source_target_pairs={{1,0},{2,1},{3,2},{5,4},{6,5},{7,6},{9,8},{10,9},{11,10},{13,12},{... | collective-permute-start | bytes 786440 | tf_op jit(solution)/shard_map/ppermute | solution.py:24
  24.7 4.0 %collective-permute-start.3 = (s32[4,8,128]{2,1,0:T(8,128)S(1)}, s32[4,8,128]{2,1,0:T(8,128)S(1)}, u32[]{:S(2)}, u32[]{:S(2)}) collective-permute-start(s32[4,8,128]{2,1,0:T(8,128)S(1)} %all_gather.3.codes_ref.codes.others), channel_id=1, source_target_pairs={{0,4},{4,0},{8,12},{12,8},{16,20},{20,16},{24,28},{28,24},{1,5},{5... | collective-permute-start | bytes 49160 | tf_op jit(solution)/shard_map/ppermute | solution.py:533
  32.4 13.4 %collective-permute-start.4 = (bf16[2,4,128,256]{3,2,1,0:T(8,128)(2,1)S(1)}, bf16[2,4,128,256]{3,2,1,0:T(8,128)(2,1)S(1)}, u32[]{:S(2)}, u32[]{:S(2)}) collective-permute-start(bf16[2,4,128,256]{3,2,1,0:T(8,128)(2,1)S(1)} %get-tuple-element.37.own), channel_id=1, source_target_pairs={{0,4},{4,8},{8,12},{12,16},{16,20},{20,24},{24,28},{1,5},{5,9},{9,... | collective-permute-start | bytes 1572872 | tf_op jit(solution)/shard_map/ppermute | solution.py:24
  35.5 10.2 %collective-permute-start.5 = (s32[8,8,128]{2,1,0:T(8,128)S(1)}, s32[8,8,128]{2,1,0:T(8,128)S(1)}, u32[]{:S(2)}, u32[]{:S(2)}) collective-permute-start(s32[8,8,128]{2,1,0:T(8,128)S(1)} %get-tuple-element.42.codes), channel_id=1, source_target_pairs={{0,8},{4,12},{8,0},{12,4},{16,24},{20,28},{24,16},{28,20},{1,9},{5... | collective-permute-start | bytes 98312 | tf_op jit(solution)/shard_map/ppermute | solution.py:533
  36.9 17.9 %copy-start.2 = (bf16[3,3,3,256,256]{4,3,2,1,0:T(8,128)(2,1)S(1)}, bf16[3,3,3,256,256]{4,3,2,1,0:T(8,128)(2,1)}, u32[]{:S(2)}) copy-start(bf16[3,3,3,256,256]{4,3,2,1,0:T(8,128)(2,1)} %weight.9) | copy-start | bytes 10616836
  46.2 12.7 %collective-permute-start.6 = (bf16[4,1,128,256]{3,2,1,0:T(8,128)(2,1)S(1)}, bf16[4,1,128,256]{3,2,1,0:T(8,128)(2,1)S(1)}, u32[]{:S(2)}, u32[]{:S(2)}) collective-permute-start(bf16[4,1,128,256]{3,2,1,0:T(8,128)(2,1)S(1)} %get-tuple-element.43), channel_id=1, source_target_pairs={{0,1},{1,2},{2,3},{4,5},{5,6},{6,7},{8,9},{9,10},{10,11},{12,13},{... | collective-permute-start | bytes 786440 | tf_op jit(solution)/shard_map/ppermute | solution.py:24
  48.5 10.5 %collective-permute-start.7 = (bf16[4,1,128,256]{3,2,1,0:T(8,128)(2,1)S(1)}, bf16[4,1,128,256]{3,2,1,0:T(8,128)(2,1)S(1)}, u32[]{:S(2)}, u32[]{:S(2)}) collective-permute-start(bf16[4,1,128,256]{3,2,1,0:T(8,128)(2,1)S(1)} %get-tuple-element.44), channel_id=1, source_target_pairs={{1,0},{2,1},{3,2},{5,4},{6,5},{7,6},{9,8},{10,9},{11,10},{13,12},{... | collective-permute-start | bytes 786440 | tf_op jit(solution)/shard_map/ppermute | solution.py:24
  50.5 8.4 %collective-permute-start.8 = (s32[16,8,128]{2,1,0:T(8,128)S(1)}, s32[16,8,128]{2,1,0:T(8,128)S(1)}, u32[]{:S(2)}, u32[]{:S(2)}) collective-permute-start(s32[16,8,128]{2,1,0:T(8,128)S(1)} %get-tuple-element.47.codes), channel_id=1, source_target_pairs={{0,16},{4,20},{8,24},{12,28},{16,0},{20,4},{24,8},{28,12},{1,17},{... | collective-permute-start | bytes 196616 | tf_op jit(solution)/shard_map/ppermute | solution.py:533
  62.0 32.3 %all-to-all-start = ((bf16[32,64,256]{2,1,0:T(8,128)(2,1)}), bf16[32,64,256]{2,1,0:T(8,128)(2,1)S(1)}, u32[]{:S(2)}, u32[]{:S(2)}) async-start(bf16[32,64,256]{2,1,0:T(8,128)(2,1)} %bitcast.7), calls=%async_computation | async-start | bytes 2097152 | tf_op jit(solution)/shard_map/all_to_all | solution.py:638
  66.0 14.5 %collective-permute-start.9 = (bf16[512,256]{1,0:T(8,128)(2,1)S(1)}, bf16[512,256]{1,0:T(8,128)(2,1)S(1)}, u32[]{:S(2)}, u32[]{:S(2)}) collective-permute-start(bf16[512,256]{1,0:T(8,128)(2,1)S(1)} %get-tuple-element.51), channel_id=1, source_target_pairs={{0,1},{1,2},{2,3},{3,0},{4,5},{5,6},{6,7},{7,4},{8,9},{9,10},{10,1... | collective-permute-start | bytes 786440 | tf_op jit(solution)/shard_map/ppermute | solution.py:29
  67.7 22.6 %collective-permute-start.10 = (bf16[512,256]{1,0:T(8,128)(2,1)S(1)}, bf16[512,256]{1,0:T(8,128)(2,1)S(1)}, u32[]{:S(2)}, u32[]{:S(2)}) collective-permute-start(bf16[512,256]{1,0:T(8,128)(2,1)S(1)} %get-tuple-element.52), channel_id=1, source_target_pairs={{0,2},{1,3},{2,0},{3,1},{4,6},{5,7},{6,4},{7,5},{8,10},{9,11},{10,... | collective-permute-start | bytes 786440 | tf_op jit(solution)/shard_map/ppermute | solution.py:29
  67.7 23.2 %collective-permute-start.11 = (bf16[512,256]{1,0:T(8,128)(2,1)S(1)}, bf16[512,256]{1,0:T(8,128)(2,1)S(1)}, u32[]{:S(2)}, u32[]{:S(2)}) collective-permute-start(bf16[512,256]{1,0:T(8,128)(2,1)S(1)} %get-tuple-element.53), channel_id=1, source_target_pairs={{0,3},{1,0},{2,1},{3,2},{4,7},{5,4},{6,5},{7,6},{8,11},{9,8},{10,9... | collective-permute-start | bytes 786440 | tf_op jit(solution)/shard_map/ppermute | solution.py:29
  68.3 22.7 %copy-start.5 = (bf16[2,4,128,256]{3,2,1,0:T(8,128)(2,1)S(1)}, bf16[2,4,128,256]{3,2,1,0:T(8,128)(2,1)}, u32[]{:S(2)}) copy-start(bf16[2,4,128,256]{3,2,1,0:T(8,128)(2,1)} %param.11) | copy-start | bytes 1572868
